TPU v7x, 32 devices: a whole 2x2x4 slice. The times are simulated.
32 devices in a mesh: cuts: 8 (over z, y), slab: 4 (over x, core).
Axes of the slice: x: 2, y: 2, z: 4, core: 2. Of those that a mesh axis runs over, the one named last changes fastest.
Arguments:
- quasi: bfloat16 [2, 48, 4, 9216], P(None, 'cuts', 'slab'), may hold values from -6 to 6
- counts: int32 [8], replicated, may hold values from 1 to 6, 16 in all
- slot_slice: int32 [48], replicated, may hold values from 0 to 15
- occupation: float32 [48], replicated, may hold values from 0.03125 to 0.25
- filter_coef: float32 [16, 9], replicated, may hold values from -2.5 to 2.5
- trap_index: int32 [4, 9216], P('slab'), may hold values from 0 to 31
- trap_table: float32 [32], replicated, may hold values from 0 to 1.5
- mean_field: float32 [4, 9216], P('slab'), may hold values from -1.5 to 0
- pairing: float32 [4, 9216], P('slab'), may hold values from 0.2 to 1
Outputs:
- normal_density: float32 [4, 9216], P('slab', 'cuts')
- anomalous_density: float32 [4, 9216], P('slab', 'cuts')
- new_mean_field: float32 [4, 9216], P('slab', 'cuts')
- new_pairing: float32 [4, 9216], P('slab', 'cuts')
Inputs may be any that keep to these rules, and one draw needn't show every extreme that they name: The live vectors of cut c fill the first counts[c] of its 6 slots; the counts sum to 16 and the largest is exactly 6.
All inputs are finite; a program needn't handle non-finite values.
Results may differ from a plain program's by a relative error of at most 0.0003.
Values may be sent and summed in bfloat16 or wider, within the bound.
A program may use at most 64 MiB of HBM per device.

v0:
```python
import jax
import jax.numpy as jnp
from jax import lax
from jax.sharding import PartitionSpec as P

NX = 96
VEC_DEV = 2
DEGREE = 8


spectral_scale = 8.5
beta_coef = 0.6
chem_level = 1.0
coupling = 1.0
density_floor = 0.05


def shifted(shard, axis, by):
    devices = lax.axis_size(axis)
    pairs = [(i, i + by) for i in range(devices) if 0 <= i + by < devices]
    return lax.ppermute(shard, axis, pairs)


def combine(field, z_lower, z_upper, y_before, y_after, potential, pairing):
    column = jnp.arange(field.shape[-1]) % NX
    left_ok = (column > 0).astype(jnp.float32)
    right_ok = (column < NX - 1).astype(jnp.float32)
    x_before = jnp.concatenate([jnp.zeros_like(field[..., :1]), field[..., :-1]], axis=3)
    x_after = jnp.concatenate([field[..., 1:], jnp.zeros_like(field[..., :1])], axis=3)
    beside_all = z_lower + z_upper + y_before + y_after
    beside_all = beside_all + x_after * right_ok + x_before * left_ok
    single = 0.5 * (6.0 * field - beside_all) + potential * field
    upper = single[0] + pairing * field[1]
    lower = pairing * field[0] - single[1]
    return jnp.stack([upper, lower]) / spectral_scale


def plane_edges(field):
    below = shifted(field, "slab", 1)
    above = shifted(field, "slab", -1)
    z_lower = jnp.concatenate([below, field[:, :, :-1]], axis=2)
    z_upper = jnp.concatenate([field[:, :, 1:], above], axis=2)
    return (z_lower, z_upper)


def remote_rows(field):
    before = shifted(field[..., -NX:], "cuts", 1)
    after = shifted(field[..., :NX], "cuts", -1)
    y_before = jnp.concatenate([before, field[..., :-NX]], axis=3)
    y_after = jnp.concatenate([field[..., NX:], after], axis=3)
    return (y_before, y_after)


def apply_block(field, potential, pairing, row_source):
    z_lower, z_upper = plane_edges(field)
    y_before, y_after = row_source(field)
    return combine(field, z_lower, z_upper, y_before, y_after, potential, pairing)


def chebyshev(vectors, coefs, operator):
    previous = vectors
    current = operator(vectors)
    filtered = (
        coefs[:, 0][None, :, None, None] * previous + coefs[:, 1][None, :, None, None] * current
    )
    for order in range(2, DEGREE + 1):
        following = 2.0 * operator(current) - previous
        filtered = filtered + coefs[:, order][None, :, None, None] * following
        previous, current = (current, following)
    return filtered


def trap_lookup(index_block, trap_table):
    levels = jnp.arange(trap_table.shape[0])
    onehot = (index_block[:, None, :] == levels[None, :, None]).astype(jnp.float32)
    return jnp.einsum("l,zlf->zf", trap_table, onehot, precision=lax.Precision.HIGHEST)


def slice_coefs(slot_ids, filter_coef):
    levels = jnp.arange(filter_coef.shape[0])
    onehot = (slot_ids[:, None] == levels[None, :]).astype(jnp.float32)
    return jnp.dot(onehot, filter_coef, precision=lax.Precision.HIGHEST)


def body(
    quasi, counts, slot_slice, occupation, filter_coef, trap_index, trap_table, mean_field, pairing
):
    cut_count = lax.axis_size("cuts")
    device = lax.axis_index("cuts")
    cap = quasi.shape[1]
    flat = quasi.shape[3]
    share = flat // cut_count
    offset = device * share
    mean_local = lax.dynamic_slice_in_dim(mean_field, offset, share, 1)
    pairing_local = lax.dynamic_slice_in_dim(pairing, offset, share, 1)
    index_local = lax.dynamic_slice_in_dim(trap_index, offset, share, 1)
    potential = trap_lookup(index_local, trap_table) + mean_local
    moved = lax.all_to_all(quasi, "cuts", split_axis=3, concat_axis=1, tiled=True)
    total_live = VEC_DEV * cut_count
    ends = jnp.cumsum(counts)
    starts = ends - counts
    global_ids = jnp.arange(total_live)
    owner = jnp.sum((ends[None, :] <= global_ids[:, None]).astype(jnp.int32), axis=1)
    owners = jnp.arange(cut_count)
    first = jnp.sum(jnp.where(owners[None, :] == owner[:, None], starts[None, :], 0), axis=1)
    row_ids = owner * cap + global_ids - first
    gathered = jnp.take(moved, row_ids, axis=1).astype(jnp.float32)
    weights = jnp.take(occupation, row_ids)
    coefs = slice_coefs(jnp.take(slot_slice, row_ids), filter_coef)

    def operator(field):
        return apply_block(field, potential, pairing_local, remote_rows)

    filtered = chebyshev(gathered, coefs, operator)
    normal = jnp.sum(weights[:, None, None] * filtered[1] * filtered[1], axis=0)
    anomal = jnp.sum(weights[:, None, None] * filtered[0] * filtered[1], axis=0)
    sums = jnp.stack([normal, anomal])
    normal_density = sums[0]
    anomalous_density = sums[1]
    cube_root = jnp.cbrt(normal_density + density_floor)
    new_mean_field = 0.5 * mean_local + 0.5 * (beta_coef * cube_root * cube_root - chem_level)
    new_pairing = 0.5 * pairing_local - coupling * anomalous_density
    return (normal_density, anomalous_density, new_mean_field, new_pairing)


def solution(mesh):
    return jax.shard_map(
        body,
        mesh=mesh,
        in_specs=(
            P(None, "cuts", "slab", None),
            P(),
            P(),
            P(),
            P(),
            P("slab", None),
            P(),
            P("slab", None),
            P("slab", None),
        ),
        out_specs=(P("slab", "cuts"), P("slab", "cuts"), P("slab", "cuts"), P("slab", "cuts")),
        check_vma=False,
    )
```

profile of v0, /device:TPU:26, one launch (start us, length us, event | category | flops | bytes accessed | tf_op | source)
XLA Modules:
  0.0 185.4 jit_solution(3026757914814294077)
XLA Ops:
  0.7 9.5 %copy.26 = bf16[2,6,1,9216]{1,0,2,3:T(2,128)(2,1)} copy(bf16[2,6,1,9216]{3,0,2,1:T(2,128)(2,1)} %param.9) | data formatting | bytes 442368 | tf_op args[0]
  10.2 9.0 %reshape.1739 = bf16[8,2,6912]{2,1,0:T(2,128)(2,1)} reshape(bf16[9216,1,2,6]{3,2,1,0:T(2,128)(2,1)} %bitcast.81) | data formatting | bytes 442368
  19.1 6.1 %all-to-all-start = ((bf16[8,2,6912]{2,1,0:T(2,128)(2,1)}), bf16[8,2,6912]{2,1,0:T(2,128)(2,1)S(1)}, u32[]{:S(2)}, u32[]{:S(2)}) async-start(bf16[8,2,6912]{2,1,0:T(2,128)(2,1)} %reshape.1739), calls=%async_computation | async-start | bytes 442368 | tf_op jit(solution)/shard_map/all_to_all | solution.py:98
  25.6 0.7 gather_fusion
  26.3 0.7 gather_fusion.1
  27.2 0.7 dynamic-slice_reduce_fusion.1
  28.0 0.9 fusion
  28.8 1.7 all-to-all-done
  30.5 11.8 %reshape.1740 = bf16[9216,1,2,6]{3,2,1,0:T(2,128)(2,1)} reshape(bf16[8,2,6912]{2,1,0:T(2,128)(2,1)S(1)} %all-to-all-done) | data formatting | bytes 442368
  42.3 7.1 %copy.30 = bf16[2,6,1,8,1152]{4,3,0,1,2:T(8,128)(2,1)S(1)} copy(bf16[2,6,1,8,1152]{1,0,4,3,2:T(2,128)(2,1)} %bitcast.80) | data formatting | bytes 442368 | tf_op jit(solution)/shard_map/all_to_all | solution.py:98
  49.6 0.7 gather_fusion.2
  50.8 1.9 %collective-permute-start = (f32[2,16,1,1152]{3,0,1,2:T(2,128)S(1)}, f32[2,16,1,1152]{3,0,1,2:T(2,128)S(1)}, u32[]{:S(2)}, u32[]{:S(2)}) collective-permute-start(f32[2,16,1,1152]{3,0,1,2:T(2,128)S(1)} %fusion.70), channel_id=1, source_target_pairs={{0,1},{1,2},{2,3},{4,5},{5,6},{6,7},{8,9},{9,10},{10,11},{12,13},{... | collective-permute-start | bytes 442376 | tf_op jit(solution)/shard_map/ppermute | solution.py:21
  52.7 3.6 %collective-permute-start.1 = (f32[2,16,1,1152]{3,0,1,2:T(2,128)S(1)}, f32[2,16,1,1152]{3,0,1,2:T(2,128)S(1)}, u32[]{:S(2)}, u32[]{:S(2)}) collective-permute-start(f32[2,16,1,1152]{3,0,1,2:T(2,128)S(1)} %fusion.70), channel_id=1, source_target_pairs={{1,0},{2,1},{3,2},{5,4},{6,5},{7,6},{9,8},{10,9},{11,10},{13,12},{... | collective-permute-start | bytes 442376 | tf_op jit(solution)/shard_map/ppermute | solution.py:21
  56.3 3.0 %collective-permute-start.3 = (f32[2,16,1,96]{3,0,1,2:T(2,128)S(1)}, f32[2,16,1,96]{3,0,1,2:T(2,128)S(1)}, u32[]{:S(2)}, u32[]{:S(2)}) collective-permute-start(f32[2,16,1,96]{3,0,1,2:T(2,128)S(1)} %get-tuple-element.67), channel_id=1, source_target_pairs={{4,0},{8,4},{12,8},{16,12},{20,16},{24,20},{28,24},{5,1},{9,5},{13... | collective-permute-start | bytes 36872 | tf_op jit(solution)/shard_map/ppermute | solution.py:21
  59.4 2.8 %collective-permute-start.2 = (f32[2,16,1,96]{3,0,1,2:T(2,128)S(1)}, f32[2,16,1,96]{3,0,1,2:T(2,128)S(1)}, u32[]{:S(2)}, u32[]{:S(2)}) collective-permute-start(f32[2,16,1,96]{3,0,1,2:T(2,128)S(1)} %get-tuple-element.66), channel_id=1, source_target_pairs={{0,4},{4,8},{8,12},{12,16},{16,20},{20,24},{24,28},{1,5},{5,9},{9,... | collective-permute-start | bytes 36872 | tf_op jit(solution)/shard_map/ppermute | solution.py:21
  62.4 3.5 %collective-permute-done.2 = f32[2,16,1,96]{3,0,1,2:T(2,128)S(1)} collective-permute-done((f32[2,16,1,96]{3,0,1,2:T(2,128)S(1)}, f32[2,16,1,96]{3,0,1,2:T(2,128)S(1)}, u32[]{:S(2)}, u32[]{:S(2)}) %collective-permute-start.2) | collective-permute-done | bytes 12320 | tf_op jit(solution)/shard_map/ppermute | solution.py:21
  65.9 0.6 multiply_add_fusion.7
  67.2 1.9 %collective-permute-start.4 = (f32[2,16,1,1152]{3,0,1,2:T(2,128)S(1)}, f32[2,16,1,1152]{3,0,1,2:T(2,128)S(1)}, u32[]{:S(2)}, u32[]{:S(2)}) collective-permute-start(f32[2,16,1,1152]{3,0,1,2:T(2,128)S(1)} %broadcast_multiply_fusion), channel_id=1, source_target_pairs={{0,1},{1,2},{2,3},{4,5},{5,6},{6,7},{8,9},{9,10},{10,11},{12,13},{... | collective-permute-start | bytes 442376 | tf_op jit(solution)/shard_map/ppermute | solution.py:21
  69.1 3.6 %collective-permute-start.5 = (f32[2,16,1,1152]{3,0,1,2:T(2,128)S(1)}, f32[2,16,1,1152]{3,0,1,2:T(2,128)S(1)}, u32[]{:S(2)}, u32[]{:S(2)}) collective-permute-start(f32[2,16,1,1152]{3,0,1,2:T(2,128)S(1)} %broadcast_multiply_fusion), channel_id=1, source_target_pairs={{1,0},{2,1},{3,2},{5,4},{6,5},{7,6},{9,8},{10,9},{11,10},{13,12},{... | collective-permute-start | bytes 442376 | tf_op jit(solution)/shard_map/ppermute | solution.py:21
  72.8 2.8 %collective-permute-start.7 = (f32[2,16,1,96]{3,0,1,2:T(2,128)S(1)}, f32[2,16,1,96]{3,0,1,2:T(2,128)S(1)}, u32[]{:S(2)}, u32[]{:S(2)}) collective-permute-start(f32[2,16,1,96]{3,0,1,2:T(2,128)S(1)} %get-tuple-element.61), channel_id=1, source_target_pairs={{4,0},{8,4},{12,8},{16,12},{20,16},{24,20},{28,24},{5,1},{9,5},{13... | collective-permute-start | bytes 36872 | tf_op jit(solution)/shard_map/ppermute | solution.py:21
  75.6 3.1 %collective-permute-start.6 = (f32[2,16,1,96]{3,0,1,2:T(2,128)S(1)}, f32[2,16,1,96]{3,0,1,2:T(2,128)S(1)}, u32[]{:S(2)}, u32[]{:S(2)}) collective-permute-start(f32[2,16,1,96]{3,0,1,2:T(2,128)S(1)} %get-tuple-element.60), channel_id=1, source_target_pairs={{0,4},{4,8},{8,12},{12,16},{16,20},{20,24},{24,28},{1,5},{5,9},{9,... | collective-permute-start | bytes 36872 | tf_op jit(solution)/shard_map/ppermute | solution.py:21
  78.9 3.2 %collective-permute-done.6 = f32[2,16,1,96]{3,0,1,2:T(2,128)S(1)} collective-permute-done((f32[2,16,1,96]{3,0,1,2:T(2,128)S(1)}, f32[2,16,1,96]{3,0,1,2:T(2,128)S(1)}, u32[]{:S(2)}, u32[]{:S(2)}) %collective-permute-start.6) | collective-permute-done | bytes 12320 | tf_op jit(solution)/shard_map/ppermute | solution.py:21
  82.1 0.5 multiply_add_fusion.6
  83.3 1.9 %collective-permute-start.8 = (f32[2,16,1,1152]{3,0,1,2:T(2,128)S(1)}, f32[2,16,1,1152]{3,0,1,2:T(2,128)S(1)}, u32[]{:S(2)}, u32[]{:S(2)}) collective-permute-start(f32[2,16,1,1152]{3,0,1,2:T(2,128)S(1)} %fusion.9), channel_id=1, source_target_pairs={{0,1},{1,2},{2,3},{4,5},{5,6},{6,7},{8,9},{9,10},{10,11},{12,13},{... | collective-permute-start | bytes 442376 | tf_op jit(solution)/shard_map/ppermute | solution.py:21
  85.3 3.6 %collective-permute-start.9 = (f32[2,16,1,1152]{3,0,1,2:T(2,128)S(1)}, f32[2,16,1,1152]{3,0,1,2:T(2,128)S(1)}, u32[]{:S(2)}, u32[]{:S(2)}) collective-permute-start(f32[2,16,1,1152]{3,0,1,2:T(2,128)S(1)} %fusion.9), channel_id=1, source_target_pairs={{1,0},{2,1},{3,2},{5,4},{6,5},{7,6},{9,8},{10,9},{11,10},{13,12},{... | collective-permute-start | bytes 442376 | tf_op jit(solution)/shard_map/ppermute | solution.py:21
  88.9 3.4 %collective-permute-start.11 = (f32[2,16,1,96]{3,0,1,2:T(2,128)S(1)}, f32[2,16,1,96]{3,0,1,2:T(2,128)S(1)}, u32[]{:S(2)}, u32[]{:S(2)}) collective-permute-start(f32[2,16,1,96]{3,0,1,2:T(2,128)S(1)} %get-tuple-element.55), channel_id=1, source_target_pairs={{4,0},{8,4},{12,8},{16,12},{20,16},{24,20},{28,24},{5,1},{9,5},{13... | collective-permute-start | bytes 36872 | tf_op jit(solution)/shard_map/ppermute | solution.py:21
  92.3 2.4 %collective-permute-start.10 = (f32[2,16,1,96]{3,0,1,2:T(2,128)S(1)}, f32[2,16,1,96]{3,0,1,2:T(2,128)S(1)}, u32[]{:S(2)}, u32[]{:S(2)}) collective-permute-start(f32[2,16,1,96]{3,0,1,2:T(2,128)S(1)} %get-tuple-element.54), channel_id=1, source_target_pairs={{0,4},{4,8},{8,12},{12,16},{16,20},{20,24},{24,28},{1,5},{5,9},{9,... | collective-permute-start | bytes 36872 | tf_op jit(solution)/shard_map/ppermute | solution.py:21
  95.0 3.8 %collective-permute-done.10 = f32[2,16,1,96]{3,0,1,2:T(2,128)S(1)} collective-permute-done((f32[2,16,1,96]{3,0,1,2:T(2,128)S(1)}, f32[2,16,1,96]{3,0,1,2:T(2,128)S(1)}, u32[]{:S(2)}, u32[]{:S(2)}) %collective-permute-start.10) | collective-permute-done | bytes 12320 | tf_op jit(solution)/shard_map/ppermute | solution.py:21
  98.9 0.6 multiply_add_fusion.5
  100.2 1.9 %collective-permute-start.12 = (f32[2,16,1,1152]{3,0,1,2:T(2,128)S(1)}, f32[2,16,1,1152]{3,0,1,2:T(2,128)S(1)}, u32[]{:S(2)}, u32[]{:S(2)}) collective-permute-start(f32[2,16,1,1152]{3,0,1,2:T(2,128)S(1)} %fusion.14), channel_id=1, source_target_pairs={{0,1},{1,2},{2,3},{4,5},{5,6},{6,7},{8,9},{9,10},{10,11},{12,13},{... | collective-permute-start | bytes 442376 | tf_op jit(solution)/shard_map/ppermute | solution.py:21
  102.2 3.6 %collective-permute-start.13 = (f32[2,16,1,1152]{3,0,1,2:T(2,128)S(1)}, f32[2,16,1,1152]{3,0,1,2:T(2,128)S(1)}, u32[]{:S(2)}, u32[]{:S(2)}) collective-permute-start(f32[2,16,1,1152]{3,0,1,2:T(2,128)S(1)} %fusion.14), channel_id=1, source_target_pairs={{1,0},{2,1},{3,2},{5,4},{6,5},{7,6},{9,8},{10,9},{11,10},{13,12},{... | collective-permute-start | bytes 442376 | tf_op jit(solution)/shard_map/ppermute | solution.py:21
  105.8 2.2 %collective-permute-start.15 = (f32[2,16,1,96]{3,0,1,2:T(2,128)S(1)}, f32[2,16,1,96]{3,0,1,2:T(2,128)S(1)}, u32[]{:S(2)}, u32[]{:S(2)}) collective-permute-start(f32[2,16,1,96]{3,0,1,2:T(2,128)S(1)} %get-tuple-element.49), channel_id=1, source_target_pairs={{4,0},{8,4},{12,8},{16,12},{20,16},{24,20},{28,24},{5,1},{9,5},{13... | collective-permute-start | bytes 36872 | tf_op jit(solution)/shard_map/ppermute | solution.py:21
  108.0 3.6 %collective-permute-start.14 = (f32[2,16,1,96]{3,0,1,2:T(2,128)S(1)}, f32[2,16,1,96]{3,0,1,2:T(2,128)S(1)}, u32[]{:S(2)}, u32[]{:S(2)}) collective-permute-start(f32[2,16,1,96]{3,0,1,2:T(2,128)S(1)} %get-tuple-element.48), channel_id=1, source_target_pairs={{0,4},{4,8},{8,12},{12,16},{16,20},{20,24},{24,28},{1,5},{5,9},{9,... | collective-permute-start | bytes 36872 | tf_op jit(solution)/shard_map/ppermute | solution.py:21
  111.9 2.7 %collective-permute-done.14 = f32[2,16,1,96]{3,0,1,2:T(2,128)S(1)} collective-permute-done((f32[2,16,1,96]{3,0,1,2:T(2,128)S(1)}, f32[2,16,1,96]{3,0,1,2:T(2,128)S(1)}, u32[]{:S(2)}, u32[]{:S(2)}) %collective-permute-start.14) | collective-permute-done | bytes 12320 | tf_op jit(solution)/shard_map/ppermute | solution.py:21
  114.6 0.7 multiply_add_fusion.4
  116.1 1.9 %collective-permute-start.16 = (f32[2,16,1,1152]{3,0,1,2:T(2,128)S(1)}, f32[2,16,1,1152]{3,0,1,2:T(2,128)S(1)}, u32[]{:S(2)}, u32[]{:S(2)}) collective-permute-start(f32[2,16,1,1152]{3,0,1,2:T(2,128)S(1)} %fusion.19), channel_id=1, source_target_pairs={{0,1},{1,2},{2,3},{4,5},{5,6},{6,7},{8,9},{9,10},{10,11},{12,13},{... | collective-permute-start | bytes 442376 | tf_op jit(solution)/shard_map/ppermute | solution.py:21
  118.0 3.8 %collective-permute-start.17 = (f32[2,16,1,1152]{3,0,1,2:T(2,128)S(1)}, f32[2,16,1,1152]{3,0,1,2:T(2,128)S(1)}, u32[]{:S(2)}, u32[]{:S(2)}) collective-permute-start(f32[2,16,1,1152]{3,0,1,2:T(2,128)S(1)} %fusion.19), channel_id=1, source_target_pairs={{1,0},{2,1},{3,2},{5,4},{6,5},{7,6},{9,8},{10,9},{11,10},{13,12},{... | collective-permute-start | bytes 442376 | tf_op jit(solution)/shard_map/ppermute | solution.py:21
  121.8 3.9 %collective-permute-start.19 = (f32[2,16,1,96]{3,0,1,2:T(2,128)S(1)}, f32[2,16,1,96]{3,0,1,2:T(2,128)S(1)}, u32[]{:S(2)}, u32[]{:S(2)}) collective-permute-start(f32[2,16,1,96]{3,0,1,2:T(2,128)S(1)} %get-tuple-element.43), channel_id=1, source_target_pairs={{4,0},{8,4},{12,8},{16,12},{20,16},{24,20},{28,24},{5,1},{9,5},{13... | collective-permute-start | bytes 36872 | tf_op jit(solution)/shard_map/ppermute | solution.py:21
  125.7 1.9 %collective-permute-start.18 = (f32[2,16,1,96]{3,0,1,2:T(2,128)S(1)}, f32[2,16,1,96]{3,0,1,2:T(2,128)S(1)}, u32[]{:S(2)}, u32[]{:S(2)}) collective-permute-start(f32[2,16,1,96]{3,0,1,2:T(2,128)S(1)} %get-tuple-element.42), channel_id=1, source_target_pairs={{0,4},{4,8},{8,12},{12,16},{16,20},{20,24},{24,28},{1,5},{5,9},{9,... | collective-permute-start | bytes 36872 | tf_op jit(solution)/shard_map/ppermute | solution.py:21
  127.9 4.4 %collective-permute-done.18 = f32[2,16,1,96]{3,0,1,2:T(2,128)S(1)} collective-permute-done((f32[2,16,1,96]{3,0,1,2:T(2,128)S(1)}, f32[2,16,1,96]{3,0,1,2:T(2,128)S(1)}, u32[]{:S(2)}, u32[]{:S(2)}) %collective-permute-start.18) | collective-permute-done | bytes 12320 | tf_op jit(solution)/shard_map/ppermute | solution.py:21
  132.3 0.7 multiply_add_fusion.3
  133.9 1.9 %collective-permute-start.20 = (f32[2,16,1,1152]{3,0,1,2:T(2,128)S(1)}, f32[2,16,1,1152]{3,0,1,2:T(2,128)S(1)}, u32[]{:S(2)}, u32[]{:S(2)}) collective-permute-start(f32[2,16,1,1152]{3,0,1,2:T(2,128)S(1)} %fusion.24), channel_id=1, source_target_pairs={{0,1},{1,2},{2,3},{4,5},{5,6},{6,7},{8,9},{9,10},{10,11},{12,13},{... | collective-permute-start | bytes 442376 | tf_op jit(solution)/shard_map/ppermute | solution.py:21
  135.9 3.6 %collective-permute-start.21 = (f32[2,16,1,1152]{3,0,1,2:T(2,128)S(1)}, f32[2,16,1,1152]{3,0,1,2:T(2,128)S(1)}, u32[]{:S(2)}, u32[]{:S(2)}) collective-permute-start(f32[2,16,1,1152]{3,0,1,2:T(2,128)S(1)} %fusion.24), channel_id=1, source_target_pairs={{1,0},{2,1},{3,2},{5,4},{6,5},{7,6},{9,8},{10,9},{11,10},{13,12},{... | collective-permute-start | bytes 442376 | tf_op jit(solution)/shard_map/ppermute | solution.py:21
  139.5 1.9 %collective-permute-start.23 = (f32[2,16,1,96]{3,0,1,2:T(2,128)S(1)}, f32[2,16,1,96]{3,0,1,2:T(2,128)S(1)}, u32[]{:S(2)}, u32[]{:S(2)}) collective-permute-start(f32[2,16,1,96]{3,0,1,2:T(2,128)S(1)} %get-tuple-element.37), channel_id=1, source_target_pairs={{4,0},{8,4},{12,8},{16,12},{20,16},{24,20},{28,24},{5,1},{9,5},{13... | collective-permute-start | bytes 36872 | tf_op jit(solution)/shard_map/ppermute | solution.py:21
  141.4 3.9 %collective-permute-start.22 = (f32[2,16,1,96]{3,0,1,2:T(2,128)S(1)}, f32[2,16,1,96]{3,0,1,2:T(2,128)S(1)}, u32[]{:S(2)}, u32[]{:S(2)}) collective-permute-start(f32[2,16,1,96]{3,0,1,2:T(2,128)S(1)} %get-tuple-element.36), channel_id=1, source_target_pairs={{0,4},{4,8},{8,12},{12,16},{16,20},{20,24},{24,28},{1,5},{5,9},{9,... | collective-permute-start | bytes 36872 | tf_op jit(solution)/shard_map/ppermute | solution.py:21
  145.6 2.4 %collective-permute-done.22 = f32[2,16,1,96]{3,0,1,2:T(2,128)S(1)} collective-permute-done((f32[2,16,1,96]{3,0,1,2:T(2,128)S(1)}, f32[2,16,1,96]{3,0,1,2:T(2,128)S(1)}, u32[]{:S(2)}, u32[]{:S(2)}) %collective-permute-start.22) | collective-permute-done | bytes 12320 | tf_op jit(solution)/shard_map/ppermute | solution.py:21
  148.0 0.8 multiply_add_fusion.2
  149.7 1.9 %collective-permute-start.24 = (f32[2,16,1,1152]{3,0,1,2:T(2,128)S(1)}, f32[2,16,1,1152]{3,0,1,2:T(2,128)S(1)}, u32[]{:S(2)}, u32[]{:S(2)}) collective-permute-start(f32[2,16,1,1152]{3,0,1,2:T(2,128)S(1)} %fusion.29), channel_id=1, source_target_pairs={{0,1},{1,2},{2,3},{4,5},{5,6},{6,7},{8,9},{9,10},{10,11},{12,13},{... | collective-permute-start | bytes 442376 | tf_op jit(solution)/shard_map/ppermute | solution.py:21
  151.7 3.6 %collective-permute-start.25 = (f32[2,16,1,1152]{3,0,1,2:T(2,128)S(1)}, f32[2,16,1,1152]{3,0,1,2:T(2,128)S(1)}, u32[]{:S(2)}, u32[]{:S(2)}) collective-permute-start(f32[2,16,1,1152]{3,0,1,2:T(2,128)S(1)} %fusion.29), channel_id=1, source_target_pairs={{1,0},{2,1},{3,2},{5,4},{6,5},{7,6},{9,8},{10,9},{11,10},{13,12},{... | collective-permute-start | bytes 442376 | tf_op jit(solution)/shard_map/ppermute | solution.py:21
  155.3 1.9 %collective-permute-start.27 = (f32[2,16,1,96]{3,0,1,2:T(2,128)S(1)}, f32[2,16,1,96]{3,0,1,2:T(2,128)S(1)}, u32[]{:S(2)}, u32[]{:S(2)}) collective-permute-start(f32[2,16,1,96]{3,0,1,2:T(2,128)S(1)} %get-tuple-element.31), channel_id=1, source_target_pairs={{4,0},{8,4},{12,8},{16,12},{20,16},{24,20},{28,24},{5,1},{9,5},{13... | collective-permute-start | bytes 36872 | tf_op jit(solution)/shard_map/ppermute | solution.py:21
  157.2 3.9 %collective-permute-start.26 = (f32[2,16,1,96]{3,0,1,2:T(2,128)S(1)}, f32[2,16,1,96]{3,0,1,2:T(2,128)S(1)}, u32[]{:S(2)}, u32[]{:S(2)}) collective-permute-start(f32[2,16,1,96]{3,0,1,2:T(2,128)S(1)} %get-tuple-element.30), channel_id=1, source_target_pairs={{0,4},{4,8},{8,12},{12,16},{16,20},{20,24},{24,28},{1,5},{5,9},{9,... | collective-permute-start | bytes 36872 | tf_op jit(solution)/shard_map/ppermute | solution.py:21
  161.4 2.4 %collective-permute-done.26 = f32[2,16,1,96]{3,0,1,2:T(2,128)S(1)} collective-permute-done((f32[2,16,1,96]{3,0,1,2:T(2,128)S(1)}, f32[2,16,1,96]{3,0,1,2:T(2,128)S(1)}, u32[]{:S(2)}, u32[]{:S(2)}) %collective-permute-start.26) | collective-permute-done | bytes 12320 | tf_op jit(solution)/shard_map/ppermute | solution.py:21
  163.8 0.9 multiply_add_fusion.1
  164.8 0.6 fusion.34
  165.7 1.9 %collective-permute-start.28 = (f32[2,16,1,1152]{3,0,1,2:T(2,128)S(1)}, f32[2,16,1,1152]{3,0,1,2:T(2,128)S(1)}, u32[]{:S(2)}, u32[]{:S(2)}) collective-permute-start(f32[2,16,1,1152]{3,0,1,2:T(2,128)S(1)} %fusion.34), channel_id=1, source_target_pairs={{0,1},{1,2},{2,3},{4,5},{5,6},{6,7},{8,9},{9,10},{10,11},{12,13},{... | collective-permute-start | bytes 442376 | tf_op jit(solution)/shard_map/ppermute | solution.py:21
  167.6 3.6 %collective-permute-start.29 = (f32[2,16,1,1152]{3,0,1,2:T(2,128)S(1)}, f32[2,16,1,1152]{3,0,1,2:T(2,128)S(1)}, u32[]{:S(2)}, u32[]{:S(2)}) collective-permute-start(f32[2,16,1,1152]{3,0,1,2:T(2,128)S(1)} %fusion.34), channel_id=1, source_target_pairs={{1,0},{2,1},{3,2},{5,4},{6,5},{7,6},{9,8},{10,9},{11,10},{13,12},{... | collective-permute-start | bytes 442376 | tf_op jit(solution)/shard_map/ppermute | solution.py:21
  171.3 1.9 %collective-permute-start.31 = (f32[2,16,1,96]{3,0,1,2:T(2,128)S(1)}, f32[2,16,1,96]{3,0,1,2:T(2,128)S(1)}, u32[]{:S(2)}, u32[]{:S(2)}) collective-permute-start(f32[2,16,1,96]{3,0,1,2:T(2,128)S(1)} %get-tuple-element.25), channel_id=1, source_target_pairs={{4,0},{8,4},{12,8},{16,12},{20,16},{24,20},{28,24},{5,1},{9,5},{13... | collective-permute-start | bytes 36872 | tf_op jit(solution)/shard_map/ppermute | solution.py:21
  173.2 3.9 %collective-permute-start.30 = (f32[2,16,1,96]{3,0,1,2:T(2,128)S(1)}, f32[2,16,1,96]{3,0,1,2:T(2,128)S(1)}, u32[]{:S(2)}, u32[]{:S(2)}) collective-permute-start(f32[2,16,1,96]{3,0,1,2:T(2,128)S(1)} %get-tuple-element.24), channel_id=1, source_target_pairs={{0,4},{4,8},{8,12},{12,16},{16,20},{20,24},{24,28},{1,5},{5,9},{9,... | collective-permute-start | bytes 36872 | tf_op jit(solution)/shard_map/ppermute | solution.py:21
  177.3 2.4 %collective-permute-done.30 = f32[2,16,1,96]{3,0,1,2:T(2,128)S(1)} collective-permute-done((f32[2,16,1,96]{3,0,1,2:T(2,128)S(1)}, f32[2,16,1,96]{3,0,1,2:T(2,128)S(1)}, u32[]{:S(2)}, u32[]{:S(2)}) %collective-permute-start.30) | collective-permute-done | bytes 12320 | tf_op jit(solution)/shard_map/ppermute | solution.py:21
  179.7 0.9 multiply_add_fusion
  180.8 1.7 fusion.41
  182.8 0.6 reduce_sum.46
  183.4 0.6 reduce_sum.48
  184.0 1.4 multiply_subtract_fusion
  (91 shorter events, 8.7 us)
Async XLA Ops:
  0.6 26.6 %copy-start = (s32[1,9216]{1,0:T(1,128)S(1)}, s32[1,9216]{1,0:T(1,128)}, u32[]{:S(2)}) copy-start(s32[1,9216]{1,0:T(1,128)} %param.14) | copy-start | bytes 110596
  0.6 24.6 %copy-start.4 = (s32[8]{0:T(128)S(1)}, s32[8]{0:T(128)}, u32[]{:S(2)}) copy-start(s32[8]{0:T(128)} %param.10) | copy-start | bytes 100
  0.7 24.9 %copy-start.1 = (f32[48]{0:T(128)S(1)}, f32[48]{0:T(128)}, u32[]{:S(2)}) copy-start(f32[48]{0:T(128)} %param.12) | copy-start | bytes 580
  0.7 25.6 %copy-start.2 = (s32[48]{0:T(128)S(1)}, s32[48]{0:T(128)}, u32[]{:S(2)}) copy-start(s32[48]{0:T(128)} %param.11) | copy-start | bytes 580
  0.7 26.3 %copy-start.3 = (f32[16,9]{1,0:T(8,128)S(1)}, f32[16,9]{1,0:T(8,128)}, u32[]{:S(2)}) copy-start(f32[16,9]{1,0:T(8,128)} %param.13) | copy-start | bytes 1732
  0.7 27.3 %copy-start.5 = (f32[32]{0:T(128)S(1)}, f32[32]{0:T(128)}, u32[]{:S(2)}) copy-start(f32[32]{0:T(128)} %param.15) | copy-start | bytes 388
  19.1 11.4 %all-to-all-start = ((bf16[8,2,6912]{2,1,0:T(2,128)(2,1)}), bf16[8,2,6912]{2,1,0:T(2,128)(2,1)S(1)}, u32[]{:S(2)}, u32[]{:S(2)}) async-start(bf16[8,2,6912]{2,1,0:T(2,128)(2,1)} %reshape.1739), calls=%async_computation | async-start | bytes 442368 | tf_op jit(solution)/shard_map/all_to_all | solution.py:98
  50.8 15.2 %collective-permute-start = (f32[2,16,1,1152]{3,0,1,2:T(2,128)S(1)}, f32[2,16,1,1152]{3,0,1,2:T(2,128)S(1)}, u32[]{:S(2)}, u32[]{:S(2)}) collective-permute-start(f32[2,16,1,1152]{3,0,1,2:T(2,128)S(1)} %fusion.70), channel_id=1, source_target_pairs={{0,1},{1,2},{2,3},{4,5},{5,6},{6,7},{8,9},{9,10},{10,11},{12,13},{... | collective-permute-start | bytes 442376 | tf_op jit(solution)/shard_map/ppermute | solution.py:21
  52.7 13.2 %collective-permute-start.1 = (f32[2,16,1,1152]{3,0,1,2:T(2,128)S(1)}, f32[2,16,1,1152]{3,0,1,2:T(2,128)S(1)}, u32[]{:S(2)}, u32[]{:S(2)}) collective-permute-start(f32[2,16,1,1152]{3,0,1,2:T(2,128)S(1)} %fusion.70), channel_id=1, source_target_pairs={{1,0},{2,1},{3,2},{5,4},{6,5},{7,6},{9,8},{10,9},{11,10},{13,12},{... | collective-permute-start | bytes 442376 | tf_op jit(solution)/shard_map/ppermute | solution.py:21
  56.3 6.1 %collective-permute-start.3 = (f32[2,16,1,96]{3,0,1,2:T(2,128)S(1)}, f32[2,16,1,96]{3,0,1,2:T(2,128)S(1)}, u32[]{:S(2)}, u32[]{:S(2)}) collective-permute-start(f32[2,16,1,96]{3,0,1,2:T(2,128)S(1)} %get-tuple-element.67), channel_id=1, source_target_pairs={{4,0},{8,4},{12,8},{16,12},{20,16},{24,20},{28,24},{5,1},{9,5},{13... | collective-permute-start | bytes 36872 | tf_op jit(solution)/shard_map/ppermute | solution.py:21
  59.4 6.5 %collective-permute-start.2 = (f32[2,16,1,96]{3,0,1,2:T(2,128)S(1)}, f32[2,16,1,96]{3,0,1,2:T(2,128)S(1)}, u32[]{:S(2)}, u32[]{:S(2)}) collective-permute-start(f32[2,16,1,96]{3,0,1,2:T(2,128)S(1)} %get-tuple-element.66), channel_id=1, source_target_pairs={{0,4},{4,8},{8,12},{12,16},{16,20},{20,24},{24,28},{1,5},{5,9},{9,... | collective-permute-start | bytes 36872 | tf_op jit(solution)/shard_map/ppermute | solution.py:21
  67.2 14.9 %collective-permute-start.4 = (f32[2,16,1,1152]{3,0,1,2:T(2,128)S(1)}, f32[2,16,1,1152]{3,0,1,2:T(2,128)S(1)}, u32[]{:S(2)}, u32[]{:S(2)}) collective-permute-start(f32[2,16,1,1152]{3,0,1,2:T(2,128)S(1)} %broadcast_multiply_fusion), channel_id=1, source_target_pairs={{0,1},{1,2},{2,3},{4,5},{5,6},{6,7},{8,9},{9,10},{10,11},{12,13},{... | collective-permute-start | bytes 442376 | tf_op jit(solution)/shard_map/ppermute | solution.py:21
  69.1 13.0 %collective-permute-start.5 = (f32[2,16,1,1152]{3,0,1,2:T(2,128)S(1)}, f32[2,16,1,1152]{3,0,1,2:T(2,128)S(1)}, u32[]{:S(2)}, u32[]{:S(2)}) collective-permute-start(f32[2,16,1,1152]{3,0,1,2:T(2,128)S(1)} %broadcast_multiply_fusion), channel_id=1, source_target_pairs={{1,0},{2,1},{3,2},{5,4},{6,5},{7,6},{9,8},{10,9},{11,10},{13,12},{... | collective-permute-start | bytes 442376 | tf_op jit(solution)/shard_map/ppermute | solution.py:21
  72.8 6.1 %collective-permute-start.7 = (f32[2,16,1,96]{3,0,1,2:T(2,128)S(1)}, f32[2,16,1,96]{3,0,1,2:T(2,128)S(1)}, u32[]{:S(2)}, u32[]{:S(2)}) collective-permute-start(f32[2,16,1,96]{3,0,1,2:T(2,128)S(1)} %get-tuple-element.61), channel_id=1, source_target_pairs={{4,0},{8,4},{12,8},{16,12},{20,16},{24,20},{28,24},{5,1},{9,5},{13... | collective-permute-start | bytes 36872 | tf_op jit(solution)/shard_map/ppermute | solution.py:21
  75.6 6.5 %collective-permute-start.6 = (f32[2,16,1,96]{3,0,1,2:T(2,128)S(1)}, f32[2,16,1,96]{3,0,1,2:T(2,128)S(1)}, u32[]{:S(2)}, u32[]{:S(2)}) collective-permute-start(f32[2,16,1,96]{3,0,1,2:T(2,128)S(1)} %get-tuple-element.60), channel_id=1, source_target_pairs={{0,4},{4,8},{8,12},{12,16},{16,20},{20,24},{24,28},{1,5},{5,9},{9,... | collective-permute-start | bytes 36872 | tf_op jit(solution)/shard_map/ppermute | solution.py:21
  83.3 15.5 %collective-permute-start.8 = (f32[2,16,1,1152]{3,0,1,2:T(2,128)S(1)}, f32[2,16,1,1152]{3,0,1,2:T(2,128)S(1)}, u32[]{:S(2)}, u32[]{:S(2)}) collective-permute-start(f32[2,16,1,1152]{3,0,1,2:T(2,128)S(1)} %fusion.9), channel_id=1, source_target_pairs={{0,1},{1,2},{2,3},{4,5},{5,6},{6,7},{8,9},{9,10},{10,11},{12,13},{... | collective-permute-start | bytes 442376 | tf_op jit(solution)/shard_map/ppermute | solution.py:21
  85.3 13.6 %collective-permute-start.9 = (f32[2,16,1,1152]{3,0,1,2:T(2,128)S(1)}, f32[2,16,1,1152]{3,0,1,2:T(2,128)S(1)}, u32[]{:S(2)}, u32[]{:S(2)}) collective-permute-start(f32[2,16,1,1152]{3,0,1,2:T(2,128)S(1)} %fusion.9), channel_id=1, source_target_pairs={{1,0},{2,1},{3,2},{5,4},{6,5},{7,6},{9,8},{10,9},{11,10},{13,12},{... | collective-permute-start | bytes 442376 | tf_op jit(solution)/shard_map/ppermute | solution.py:21
  88.9 6.1 %collective-permute-start.11 = (f32[2,16,1,96]{3,0,1,2:T(2,128)S(1)}, f32[2,16,1,96]{3,0,1,2:T(2,128)S(1)}, u32[]{:S(2)}, u32[]{:S(2)}) collective-permute-start(f32[2,16,1,96]{3,0,1,2:T(2,128)S(1)} %get-tuple-element.55), channel_id=1, source_target_pairs={{4,0},{8,4},{12,8},{16,12},{20,16},{24,20},{28,24},{5,1},{9,5},{13... | collective-permute-start | bytes 36872 | tf_op jit(solution)/shard_map/ppermute | solution.py:21
  92.3 6.5 %collective-permute-start.10 = (f32[2,16,1,96]{3,0,1,2:T(2,128)S(1)}, f32[2,16,1,96]{3,0,1,2:T(2,128)S(1)}, u32[]{:S(2)}, u32[]{:S(2)}) collective-permute-start(f32[2,16,1,96]{3,0,1,2:T(2,128)S(1)} %get-tuple-element.54), channel_id=1, source_target_pairs={{0,4},{4,8},{8,12},{12,16},{16,20},{20,24},{24,28},{1,5},{5,9},{9,... | collective-permute-start | bytes 36872 | tf_op jit(solution)/shard_map/ppermute | solution.py:21
  100.2 14.3 %collective-permute-start.12 = (f32[2,16,1,1152]{3,0,1,2:T(2,128)S(1)}, f32[2,16,1,1152]{3,0,1,2:T(2,128)S(1)}, u32[]{:S(2)}, u32[]{:S(2)}) collective-permute-start(f32[2,16,1,1152]{3,0,1,2:T(2,128)S(1)} %fusion.14), channel_id=1, source_target_pairs={{0,1},{1,2},{2,3},{4,5},{5,6},{6,7},{8,9},{9,10},{10,11},{12,13},{... | collective-permute-start | bytes 442376 | tf_op jit(solution)/shard_map/ppermute | solution.py:21
  102.2 12.4 %collective-permute-start.13 = (f32[2,16,1,1152]{3,0,1,2:T(2,128)S(1)}, f32[2,16,1,1152]{3,0,1,2:T(2,128)S(1)}, u32[]{:S(2)}, u32[]{:S(2)}) collective-permute-start(f32[2,16,1,1152]{3,0,1,2:T(2,128)S(1)} %fusion.14), channel_id=1, source_target_pairs={{1,0},{2,1},{3,2},{5,4},{6,5},{7,6},{9,8},{10,9},{11,10},{13,12},{... | collective-permute-start | bytes 442376 | tf_op jit(solution)/shard_map/ppermute | solution.py:21
  105.8 6.1 %collective-permute-start.15 = (f32[2,16,1,96]{3,0,1,2:T(2,128)S(1)}, f32[2,16,1,96]{3,0,1,2:T(2,128)S(1)}, u32[]{:S(2)}, u32[]{:S(2)}) collective-permute-start(f32[2,16,1,96]{3,0,1,2:T(2,128)S(1)} %get-tuple-element.49), channel_id=1, source_target_pairs={{4,0},{8,4},{12,8},{16,12},{20,16},{24,20},{28,24},{5,1},{9,5},{13... | collective-permute-start | bytes 36872 | tf_op jit(solution)/shard_map/ppermute | solution.py:21
  108.0 6.5 %collective-permute-start.14 = (f32[2,16,1,96]{3,0,1,2:T(2,128)S(1)}, f32[2,16,1,96]{3,0,1,2:T(2,128)S(1)}, u32[]{:S(2)}, u32[]{:S(2)}) collective-permute-start(f32[2,16,1,96]{3,0,1,2:T(2,128)S(1)} %get-tuple-element.48), channel_id=1, source_target_pairs={{0,4},{4,8},{8,12},{12,16},{16,20},{20,24},{24,28},{1,5},{5,9},{9,... | collective-permute-start | bytes 36872 | tf_op jit(solution)/shard_map/ppermute | solution.py:21
  116.1 16.2 %collective-permute-start.16 = (f32[2,16,1,1152]{3,0,1,2:T(2,128)S(1)}, f32[2,16,1,1152]{3,0,1,2:T(2,128)S(1)}, u32[]{:S(2)}, u32[]{:S(2)}) collective-permute-start(f32[2,16,1,1152]{3,0,1,2:T(2,128)S(1)} %fusion.19), channel_id=1, source_target_pairs={{0,1},{1,2},{2,3},{4,5},{5,6},{6,7},{8,9},{9,10},{10,11},{12,13},{... | collective-permute-start | bytes 442376 | tf_op jit(solution)/shard_map/ppermute | solution.py:21
  118.0 14.3 %collective-permute-start.17 = (f32[2,16,1,1152]{3,0,1,2:T(2,128)S(1)}, f32[2,16,1,1152]{3,0,1,2:T(2,128)S(1)}, u32[]{:S(2)}, u32[]{:S(2)}) collective-permute-start(f32[2,16,1,1152]{3,0,1,2:T(2,128)S(1)} %fusion.19), channel_id=1, source_target_pairs={{1,0},{2,1},{3,2},{5,4},{6,5},{7,6},{9,8},{10,9},{11,10},{13,12},{... | collective-permute-start | bytes 442376 | tf_op jit(solution)/shard_map/ppermute | solution.py:21
  121.8 6.1 %collective-permute-start.19 = (f32[2,16,1,96]{3,0,1,2:T(2,128)S(1)}, f32[2,16,1,96]{3,0,1,2:T(2,128)S(1)}, u32[]{:S(2)}, u32[]{:S(2)}) collective-permute-start(f32[2,16,1,96]{3,0,1,2:T(2,128)S(1)} %get-tuple-element.43), channel_id=1, source_target_pairs={{4,0},{8,4},{12,8},{16,12},{20,16},{24,20},{28,24},{5,1},{9,5},{13... | collective-permute-start | bytes 36872 | tf_op jit(solution)/shard_map/ppermute | solution.py:21
  125.7 6.5 %collective-permute-start.18 = (f32[2,16,1,96]{3,0,1,2:T(2,128)S(1)}, f32[2,16,1,96]{3,0,1,2:T(2,128)S(1)}, u32[]{:S(2)}, u32[]{:S(2)}) collective-permute-start(f32[2,16,1,96]{3,0,1,2:T(2,128)S(1)} %get-tuple-element.42), channel_id=1, source_target_pairs={{0,4},{4,8},{8,12},{12,16},{16,20},{20,24},{24,28},{1,5},{5,9},{9,... | collective-permute-start | bytes 36872 | tf_op jit(solution)/shard_map/ppermute | solution.py:21
  133.9 14.0 %collective-permute-start.20 = (f32[2,16,1,1152]{3,0,1,2:T(2,128)S(1)}, f32[2,16,1,1152]{3,0,1,2:T(2,128)S(1)}, u32[]{:S(2)}, u32[]{:S(2)}) collective-permute-start(f32[2,16,1,1152]{3,0,1,2:T(2,128)S(1)} %fusion.24), channel_id=1, source_target_pairs={{0,1},{1,2},{2,3},{4,5},{5,6},{6,7},{8,9},{9,10},{10,11},{12,13},{... | collective-permute-start | bytes 442376 | tf_op jit(solution)/shard_map/ppermute | solution.py:21
  135.9 12.1 %collective-permute-start.21 = (f32[2,16,1,1152]{3,0,1,2:T(2,128)S(1)}, f32[2,16,1,1152]{3,0,1,2:T(2,128)S(1)}, u32[]{:S(2)}, u32[]{:S(2)}) collective-permute-start(f32[2,16,1,1152]{3,0,1,2:T(2,128)S(1)} %fusion.24), channel_id=1, source_target_pairs={{1,0},{2,1},{3,2},{5,4},{6,5},{7,6},{9,8},{10,9},{11,10},{13,12},{... | collective-permute-start | bytes 442376 | tf_op jit(solution)/shard_map/ppermute | solution.py:21
  139.5 6.1 %collective-permute-start.23 = (f32[2,16,1,96]{3,0,1,2:T(2,128)S(1)}, f32[2,16,1,96]{3,0,1,2:T(2,128)S(1)}, u32[]{:S(2)}, u32[]{:S(2)}) collective-permute-start(f32[2,16,1,96]{3,0,1,2:T(2,128)S(1)} %get-tuple-element.37), channel_id=1, source_target_pairs={{4,0},{8,4},{12,8},{16,12},{20,16},{24,20},{28,24},{5,1},{9,5},{13... | collective-permute-start | bytes 36872 | tf_op jit(solution)/shard_map/ppermute | solution.py:21
  141.4 6.5 %collective-permute-start.22 = (f32[2,16,1,96]{3,0,1,2:T(2,128)S(1)}, f32[2,16,1,96]{3,0,1,2:T(2,128)S(1)}, u32[]{:S(2)}, u32[]{:S(2)}) collective-permute-start(f32[2,16,1,96]{3,0,1,2:T(2,128)S(1)} %get-tuple-element.36), channel_id=1, source_target_pairs={{0,4},{4,8},{8,12},{12,16},{16,20},{20,24},{24,28},{1,5},{5,9},{9,... | collective-permute-start | bytes 36872 | tf_op jit(solution)/shard_map/ppermute | solution.py:21
  149.7 14.0 %collective-permute-start.24 = (f32[2,16,1,1152]{3,0,1,2:T(2,128)S(1)}, f32[2,16,1,1152]{3,0,1,2:T(2,128)S(1)}, u32[]{:S(2)}, u32[]{:S(2)}) collective-permute-start(f32[2,16,1,1152]{3,0,1,2:T(2,128)S(1)} %fusion.29), channel_id=1, source_target_pairs={{0,1},{1,2},{2,3},{4,5},{5,6},{6,7},{8,9},{9,10},{10,11},{12,13},{... | collective-permute-start | bytes 442376 | tf_op jit(solution)/shard_map/ppermute | solution.py:21
  151.7 12.1 %collective-permute-start.25 = (f32[2,16,1,1152]{3,0,1,2:T(2,128)S(1)}, f32[2,16,1,1152]{3,0,1,2:T(2,128)S(1)}, u32[]{:S(2)}, u32[]{:S(2)}) collective-permute-start(f32[2,16,1,1152]{3,0,1,2:T(2,128)S(1)} %fusion.29), channel_id=1, source_target_pairs={{1,0},{2,1},{3,2},{5,4},{6,5},{7,6},{9,8},{10,9},{11,10},{13,12},{... | collective-permute-start | bytes 442376 | tf_op jit(solution)/shard_map/ppermute | solution.py:21
  155.3 6.1 %collective-permute-start.27 = (f32[2,16,1,96]{3,0,1,2:T(2,128)S(1)}, f32[2,16,1,96]{3,0,1,2:T(2,128)S(1)}, u32[]{:S(2)}, u32[]{:S(2)}) collective-permute-start(f32[2,16,1,96]{3,0,1,2:T(2,128)S(1)} %get-tuple-element.31), channel_id=1, source_target_pairs={{4,0},{8,4},{12,8},{16,12},{20,16},{24,20},{28,24},{5,1},{9,5},{13... | collective-permute-start | bytes 36872 | tf_op jit(solution)/shard_map/ppermute | solution.py:21
  157.2 6.5 %collective-permute-start.26 = (f32[2,16,1,96]{3,0,1,2:T(2,128)S(1)}, f32[2,16,1,96]{3,0,1,2:T(2,128)S(1)}, u32[]{:S(2)}, u32[]{:S(2)}) collective-permute-start(f32[2,16,1,96]{3,0,1,2:T(2,128)S(1)} %get-tuple-element.30), channel_id=1, source_target_pairs={{0,4},{4,8},{8,12},{12,16},{16,20},{20,24},{24,28},{1,5},{5,9},{9,... | collective-permute-start | bytes 36872 | tf_op jit(solution)/shard_map/ppermute | solution.py:21
  165.7 14.0 %collective-permute-start.28 = (f32[2,16,1,1152]{3,0,1,2:T(2,128)S(1)}, f32[2,16,1,1152]{3,0,1,2:T(2,128)S(1)}, u32[]{:S(2)}, u32[]{:S(2)}) collective-permute-start(f32[2,16,1,1152]{3,0,1,2:T(2,128)S(1)} %fusion.34), channel_id=1, source_target_pairs={{0,1},{1,2},{2,3},{4,5},{5,6},{6,7},{8,9},{9,10},{10,11},{12,13},{... | collective-permute-start | bytes 442376 | tf_op jit(solution)/shard_map/ppermute | solution.py:21
  167.6 12.1 %collective-permute-start.29 = (f32[2,16,1,1152]{3,0,1,2:T(2,128)S(1)}, f32[2,16,1,1152]{3,0,1,2:T(2,128)S(1)}, u32[]{:S(2)}, u32[]{:S(2)}) collective-permute-start(f32[2,16,1,1152]{3,0,1,2:T(2,128)S(1)} %fusion.34), channel_id=1, source_target_pairs={{1,0},{2,1},{3,2},{5,4},{6,5},{7,6},{9,8},{10,9},{11,10},{13,12},{... | collective-permute-start | bytes 442376 | tf_op jit(solution)/shard_map/ppermute | solution.py:21
  171.3 6.1 %collective-permute-start.31 = (f32[2,16,1,96]{3,0,1,2:T(2,128)S(1)}, f32[2,16,1,96]{3,0,1,2:T(2,128)S(1)}, u32[]{:S(2)}, u32[]{:S(2)}) collective-permute-start(f32[2,16,1,96]{3,0,1,2:T(2,128)S(1)} %get-tuple-element.25), channel_id=1, source_target_pairs={{4,0},{8,4},{12,8},{16,12},{20,16},{24,20},{28,24},{5,1},{9,5},{13... | collective-permute-start | bytes 36872 | tf_op jit(solution)/shard_map/ppermute | solution.py:21
  173.2 6.5 %collective-permute-start.30 = (f32[2,16,1,96]{3,0,1,2:T(2,128)S(1)}, f32[2,16,1,96]{3,0,1,2:T(2,128)S(1)}, u32[]{:S(2)}, u32[]{:S(2)}) collective-permute-start(f32[2,16,1,96]{3,0,1,2:T(2,128)S(1)} %get-tuple-element.24), channel_id=1, source_target_pairs={{0,4},{4,8},{8,12},{12,16},{16,20},{20,24},{24,28},{1,5},{5,9},{9,... | collective-permute-start | bytes 36872 | tf_op jit(solution)/shard_map/ppermute | solution.py:21
where the time goes:
time: 187 us; the launch traced here: 185 us
  starting transfers between devices  97.4 us (52%)
  local copies, waits for them, and re-layouts  45.6 us (24%)
  waiting for transfers between devices  26.5 us (14%)
  other arithmetic  13.5 us (7%)
    ppermute x32, starting transfers between devices, shifted(): return lax.ppermute(shard, axis, pairs)  91.4 us
    unnamed x15, local copies, waits for them, and re-layouts  30.2 us
    ppermute x32, waiting for transfers between devices, shifted(): return lax.ppermute(shard, axis, pairs)  24.8 us
    all_to_all x2, local copies, waits for them, and re-layouts, body(): lax.all_to_all(quasi, 'cuts', split_axis=3, concat_axis=1, tiled=True)  7.29 us
    all_to_all x1, starting transfers between devices, body(): lax.all_to_all(quasi, 'cuts', split_axis=3, concat_axis=1, tiled=True)  6.05 us
    add x8, other arithmetic, combine(): single = 0.5 * (6.0 * field - beside_all) + potential * field  5.74 us
  transfers between devices with their start and end apart: 33, of which 9 were waited for; matrix products, arithmetic and copies ran while one was open for 3% of the time, Pallas kernels for 0%

commit v1 on v0

v1 whole, which is shorter than its diff:
```python
import functools

import jax
import jax.numpy as jnp
from jax import lax
from jax.experimental import pallas as pl
from jax.experimental.pallas import tpu as pltpu
from jax.sharding import PartitionSpec as P

NX = 96
DEGREE = 8
LANES = 128
PACK = 4
FLAT = 3
TILE = 16

spectral_scale = 8.5
beta_coef = 0.6
chem_level = 1.0
coupling = 1.0
density_floor = 0.05

MESH = pl.DeviceIdType.MESH


def round_up(value, step):
    return -(-value // step) * step


def plan(n_cuts, n_slab, cap, flat):
    groups = 2 if cap % 2 == 0 and n_slab % 2 == 0 else 1
    pieces = n_slab // groups
    total = flat // (NX * PACK)
    core = total // pieces
    halo = -(-DEGREE // PACK)
    width = min(round_up(core + 2 * halo, TILE), round_up(total, TILE))
    if total >= TILE and core + halo <= TILE:
        width = TILE if pieces <= 2 else width
    starts = [min(max(piece * core - halo, 0), total - width) for piece in range(pieces)]
    return groups, pieces, core, width, starts


def for_planes(count, body):
    chunk = 4 if count % 4 == 0 else 1
    if count == chunk:
        for z in range(chunk):
            body(z)
        return

    def some(i, carry):
        for z in range(chunk):
            body(i * chunk + z)
        return carry

    lax.fori_loop(0, count // chunk, some, 0)


def to_rows(flat_rows, lane):
    p0, p1, p2 = flat_rows
    r0, r1 = pltpu.roll(p0, 32, 1), pltpu.roll(p1, 32, 1)
    s1, s2 = pltpu.roll(p1, 64, 1), pltpu.roll(p2, 64, 1)
    rows = [
        p0,
        jnp.where(lane < 32, r0, r1),
        jnp.where(lane < 64, s1, s2),
        pltpu.roll(p2, 96, 1),
    ]
    return [jnp.where(lane < NX, row, 0.0) for row in rows]


def kernel(
    dims,
    counts,
    slot_slice,
    occupation,
    coef,
    vectors,
    fields,
    out,
    got_q,
    got_f,
    q_rows,
    ab,
    even,
    odd,
    dens,
    parts,
    landed,
    q_send,
    q_recv,
    f_send,
    f_recv,
    p_send,
    p_recv,
):
    n_cuts, nz, groups, pieces, core, width, starts, per_group, share_rows = dims
    cut, slab = lax.axis_index("cuts"), lax.axis_index("slab")
    piece, group = slab // groups, slab % groups
    near = n_cuts // pieces
    home = cut // near
    cap = per_group * groups
    mine = cut * groups + group
    n_sources = n_cuts * groups
    n_targets = near * nz
    keeps_own = (home == piece).astype(jnp.int32)

    barrier = pltpu.get_barrier_semaphore()
    for o in range(1, nz):
        pl.semaphore_signal(
            barrier, inc=1, device_id=(cut, (slab + o) % nz), device_id_type=MESH
        )

    def greet(i, carry):
        source = (mine + i) % n_sources
        c, s = source // groups, home * groups + source % groups

        @pl.when(jnp.logical_or(c != cut, s != slab))
        def _():
            pl.semaphore_signal(barrier, inc=1, device_id=(c, s), device_id_type=MESH)

        return carry

    lax.fori_loop(0, n_sources, greet, 0)
    pl.semaphore_wait(barrier, nz - 1 + n_targets - keeps_own)

    def field_copy(to):
        return pltpu.make_async_remote_copy(
            src_ref=fields.at[to // groups],
            dst_ref=got_f.at[slab],
            send_sem=f_send.at[to],
            recv_sem=f_recv.at[slab],
            device_id=(cut, to),
            device_id_type=MESH,
        )

    def vector_copy(to, slot):
        return pltpu.make_async_remote_copy(
            src_ref=vectors.at[to // groups, to % groups, slot],
            dst_ref=got_q.at[slot, slab],
            send_sem=q_send.at[slot, to],
            recv_sem=q_recv.at[slot, slab],
            device_id=(cut, to),
            device_id_type=MESH,
        )

    others = [(slab + o) % nz for o in range(1, nz)]
    for to in others:
        field_copy(to).start()
        vector_copy(to, 0).start()
    own_f = pltpu.make_async_copy(fields.at[piece], got_f.at[slab], f_recv.at[slab])
    own_f.start()

    def own_q(slot):
        return pltpu.make_async_copy(
            vectors.at[piece, group, slot], got_q.at[slot, slab], q_recv.at[slot, slab]
        )

    own_q(0).start()
    for slot in range(1, per_group):
        for to in others:
            vector_copy(to, slot).start()
        own_q(slot).start()

    lane = lax.broadcasted_iota(jnp.int32, (width, LANES), 1)
    line = lax.broadcasted_iota(jnp.int32, (width, LANES), 0)
    not_first, not_last = line > 0, line < width - 1
    hop = jnp.where(lane < NX, -1.0 / spectral_scale, 0.0).astype(jnp.float32)

    blank = jnp.zeros((2, PACK, width, LANES), jnp.float32)
    for buffer in (even, odd):
        buffer[:, 0] = blank
        buffer[:, nz + 1] = blank
    dens[...] = jnp.zeros(dens.shape, jnp.float32)

    def wait_fields(src):
        pltpu.make_async_remote_copy(
            src_ref=fields.at[piece],
            dst_ref=got_f.at[src],
            send_sem=f_send.at[src],
            recv_sem=f_recv.at[src],
            device_id=(cut, src),
            device_id_type=MESH,
        ).wait_recv()

    own_f.wait()
    for src in others:
        wait_fields(src)

    def unpack_fields(z):
        for which in range(2):
            rows = to_rows([got_f[z, which, j] for j in range(FLAT)], lane)
            for i in range(PACK):
                ab[which, z, i] = rows[i]

    for_planes(nz, unpack_fields)

    def beside(ref, part, z):
        rows = [ref[part, z + 1, i] for i in range(PACK)]
        above = jnp.where(not_first, pltpu.roll(rows[-1], 1, 0), 0.0)
        below = jnp.where(not_last, pltpu.roll(rows[0], width - 1, 0), 0.0)
        padded = [above] + rows + [below]
        sums = []
        for i in range(PACK):
            around = pltpu.roll(rows[i], 1, 1) + pltpu.roll(rows[i], LANES - 1, 1)
            around = around + (padded[i] + padded[i + 2])
            around = around + (ref[part, z, i] + ref[part, z + 2, i])
            sums.append(hop * around)
        return rows, sums

    def twice_operator(ref, z):
        u, near_u = beside(ref, 0, z)
        v, near_v = beside(ref, 1, z)
        results = []
        for i in range(PACK):
            a, b = ab[0, z, i], ab[1, z, i]
            results.append((a * u[i] + b * v[i] + near_u[i], b * u[i] - a * v[i] - near_v[i]))
        return results

    def clenshaw(now, then, scale, first=False):
        def plane(z):
            for i, pair in enumerate(twice_operator(now, z)):
                for part in range(2):
                    value = scale * q_rows[part, z, i] + pair[part]
                    if not first:
                        value = value - then[part, z + 1, i]
                    then[part, z + 1, i] = value

        for_planes(nz, plane)

    def one_slot(slot, carry):
        own_q(slot).wait()
        for src in others:
            pltpu.make_async_remote_copy(
                src_ref=vectors.at[piece, group, slot],
                dst_ref=got_q.at[slot, src],
                send_sem=q_send.at[slot, src],
                recv_sem=q_recv.at[slot, src],
                device_id=(cut, src),
                device_id_type=MESH,
            ).wait_recv()
        index = group * per_group + slot
        number = cut * cap + index
        level = slot_slice[number]
        weight = jnp.where(index < counts[cut], occupation[number], 0.0)
        last = coef[level, DEGREE]

        def unpack(z):
            for part in range(2):
                flat = [got_q[slot, z, j, part].astype(jnp.float32) for j in range(FLAT)]
                rows = to_rows(flat, lane)
                for i in range(PACK):
                    q_rows[part, z, i] = rows[i]
                    even[part, z + 1, i] = last * rows[i]

        for_planes(nz, unpack)
        clenshaw(even, odd, coef[level, DEGREE - 1], first=True)

        def two_steps(k, inner):
            order = DEGREE - 2 - 2 * k
            clenshaw(odd, even, coef[level, order])
            clenshaw(even, odd, coef[level, order - 1])
            return inner

        lax.fori_loop(0, (DEGREE - 2) // 2, two_steps, 0)
        base = coef[level, 0]

        def finish(z):
            for i, pair in enumerate(twice_operator(odd, z)):
                f = [
                    base * q_rows[part, z, i] + 0.5 * pair[part] - even[part, z + 1, i]
                    for part in range(2)
                ]
                heavy = weight * f[1]
                dens[0, z, i] += heavy * f[1]
                dens[1, z, i] += heavy * f[0]

        for_planes(nz, finish)
        return carry

    lax.fori_loop(0, per_group, one_slot, 0)

    start = jnp.int32(starts[0])
    for p in range(1, pieces):
        start = jnp.where(piece == p, starts[p], start)
    inside = piece * core - start

    def pack(z):
        for c in range(near):
            for r in range(share_rows):
                y = c * share_rows + r
                for which in range(2):
                    parts[c, z, pl.ds(which * share_rows + r, 1)] = dens[
                        which, z, y % PACK, pl.ds(inside + y // PACK, 1)
                    ]

    for_planes(nz, pack)

    def part_copy(c, z):
        return pltpu.make_async_remote_copy(
            src_ref=parts.at[c, z],
            dst_ref=landed.at[mine],
            send_sem=p_send.at[c, z],
            recv_sem=p_recv.at[mine],
            device_id=(piece * near + c, z),
            device_id_type=MESH,
        )

    def each_target(act):
        def body(t, carry):
            c, z = (t + cut) % near, (t // near + slab) % nz
            elsewhere = jnp.logical_or(piece * near + c != cut, z != slab)

            @pl.when(elsewhere)
            def _():
                act(part_copy(c, z))

            return carry

        lax.fori_loop(0, n_targets, body, 0)

    each_target(lambda copy: copy.start())

    @pl.when(home == piece)
    def _():
        landed[mine] = parts[cut % near, slab]

    def arrivals(i, carry):
        source = (mine + i) % n_sources
        c, s = source // groups, home * groups + source % groups

        @pl.when(jnp.logical_or(c != cut, s != slab))
        def _():
            pltpu.make_async_remote_copy(
                src_ref=parts.at[0, 0],
                dst_ref=landed.at[source],
                send_sem=p_send.at[0, 0],
                recv_sem=p_recv.at[source],
                device_id=(c, s),
                device_id_type=MESH,
            ).wait_recv()

        return carry

    lax.fori_loop(0, n_sources, arrivals, 0)
    total = landed[0]
    for source in range(1, n_sources):
        total = total + landed[source]
    out[...] = total

    for to in others:
        field_copy(to).wait_send()
        for slot in range(per_group):
            vector_copy(to, slot).wait_send()
    each_target(lambda copy: copy.wait_send())


def body(
    quasi, counts, slot_slice, occupation, filter_coef, trap_index, trap_table, mean_field, pairing
):
    n_cuts, nz = lax.axis_size("cuts"), lax.axis_size("slab")
    cut = lax.axis_index("cuts")
    cap, flat = quasi.shape[1], quasi.shape[3]
    share = flat // n_cuts
    share_rows = share // NX
    groups, pieces, core, width, starts = plan(n_cuts, nz, cap, flat)
    per_group = cap // groups
    n_groups = flat // (NX * PACK)

    levels = jnp.arange(trap_table.shape[0])
    hit = trap_index[None] == levels[:, None, None]
    trap = jnp.sum(jnp.where(hit, trap_table[:, None, None], 0.0), axis=0)
    diagonal = (2.0 / spectral_scale) * (3.0 + trap + mean_field)
    both = jnp.concatenate([diagonal, (2.0 / spectral_scale) * pairing], axis=0)
    both = both.reshape(2, n_groups, FLAT, LANES).transpose(0, 2, 1, 3)
    fields = jnp.stack([both[:, :, s : s + width] for s in starts])

    q = quasi.reshape(2, groups, per_group, n_groups, FLAT, LANES)
    q = q.transpose(1, 2, 4, 0, 3, 5)
    vectors = jnp.stack([q[:, :, :, :, s : s + width] for s in starts])

    rows = round_up(2 * share_rows, 8)
    near = n_cuts // pieces
    dims = (n_cuts, nz, groups, pieces, core, width, starts, per_group, share_rows)
    f32 = jnp.float32
    sums = pl.pallas_call(
        functools.partial(kernel, dims),
        out_shape=jax.ShapeDtypeStruct((rows, LANES), f32),
        in_specs=[pl.BlockSpec(memory_space=pltpu.SMEM)] * 4
        + [pl.BlockSpec(memory_space=pl.ANY)] * 2,
        out_specs=pl.BlockSpec(memory_space=pltpu.VMEM),
        scratch_shapes=[
            pltpu.VMEM((per_group, nz, FLAT, 2, width, LANES), jnp.bfloat16),
            pltpu.VMEM((nz, 2, FLAT, width, LANES), f32),
            pltpu.VMEM((2, nz, PACK, width, LANES), f32),
            pltpu.VMEM((2, nz, PACK, width, LANES), f32),
            pltpu.VMEM((2, nz + 2, PACK, width, LANES), f32),
            pltpu.VMEM((2, nz + 2, PACK, width, LANES), f32),
            pltpu.VMEM((2, nz, PACK, width, LANES), f32),
            pltpu.VMEM((near, nz, rows, LANES), f32),
            pltpu.VMEM((n_cuts * groups, rows, LANES), f32),
            pltpu.SemaphoreType.DMA((per_group, nz)),
            pltpu.SemaphoreType.DMA((per_group, nz)),
            pltpu.SemaphoreType.DMA((nz,)),
            pltpu.SemaphoreType.DMA((nz,)),
            pltpu.SemaphoreType.DMA((near, nz)),
            pltpu.SemaphoreType.DMA((n_cuts * groups,)),
        ],
        compiler_params=pltpu.CompilerParams(
            collective_id=0, has_side_effects=True, vmem_limit_bytes=48 * 1024 * 1024
        ),
    )(counts, slot_slice, occupation, filter_coef, vectors, fields)

    normal_density = sums[:share_rows, :NX].reshape(1, share)
    anomalous_density = sums[share_rows : 2 * share_rows, :NX].reshape(1, share)
    mean_local = lax.dynamic_slice_in_dim(mean_field, cut * share, share, 1)
    pairing_local = lax.dynamic_slice_in_dim(pairing, cut * share, share, 1)
    cube_root = jnp.cbrt(normal_density + density_floor)
    new_mean_field = 0.5 * mean_local + 0.5 * (beta_coef * cube_root * cube_root - chem_level)
    new_pairing = 0.5 * pairing_local - coupling * anomalous_density
    return (normal_density, anomalous_density, new_mean_field, new_pairing)


def solution(mesh):
    return jax.shard_map(
        body,
        mesh=mesh,
        in_specs=(
            P(None, "cuts", "slab", None),
            P(),
            P(),
            P(),
            P(),
            P("slab", None),
            P(),
            P("slab", None),
            P("slab", None),
        ),
        out_specs=(P("slab", "cuts"), P("slab", "cuts"), P("slab", "cuts"), P("slab", "cuts")),
        check_vma=False,
    )
```

time: 187 us -> 33.7 us (0.18)
  the two profiles are of different devices: /device:TPU:26 before, /device:TPU:0 now
where the time goes in v1:
time: 33.7 us; the launch traced here: 33.5 us
  Pallas kernels  28.1 us (83%)
  local copies, waits for them, and re-layouts  2.81 us (8%)
  other arithmetic  1.73 us (5%)
  between operations  0.82 us (2%)
    pallas_call x1, Pallas kernels, body(): pl.pallas_call(functools.partial(kernel, dims), out_shape=jax.ShapeDtypeS...  28.1 us
    unnamed x20, local copies, waits for them, and re-layouts  1.34 us
    reshape x2, local copies, waits for them, and re-layouts, body(): q = quasi.reshape(2, groups, per_group, n_groups, FLAT, LANES)  1.16 us

profile of v1, /device:TPU:0, one launch (start us, length us, event | category | flops | bytes accessed | tf_op | source)
XLA Modules:
  0.0 33.5 jit_solution(13514435882031444546)
XLA Ops:
  0.6 1.1 %reshape.121 = bf16[2,2,3,24,3,128]{5,4,3,0,2,1:T(4,128)(2,1)S(1)} reshape(bf16[2,6,1,9216]{3,0,2,1:T(2,128)(2,1)} %param.9) | data formatting | bytes 442368 | tf_op jit(solution)/shard_map/reshape | solution.py:377
  1.9 0.0 copy-start.6
  1.9 0.0 copy-start.9
  1.9 0.0 copy-start.4
  1.9 0.0 copy-start.5
  1.9 0.7 %copy-done.6 = s32[1,9216]{1,0:T(1,128)S(1)} copy-done((s32[1,9216]{1,0:T(1,128)S(1)}, s32[1,9216]{1,0:T(1,128)}, u32[]{:S(2)}) %copy-start.6) | copy-done | bytes 36888
  2.6 0.0 copy-done.9
  2.6 0.3 select_reduce_fusion
  2.9 0.0 copy-done.4
  2.9 0.0 copy-done.5
  2.9 0.1 add_multiply_fusion
  3.0 0.1 pad_maximum_fusion.2
  3.1 0.1 reshape.122
  3.2 0.0 copy-start
  3.2 0.0 copy-start.1
  3.2 0.0 copy-start.2
  3.2 0.0 copy-start.3
  3.3 0.6 %copy-done = f32[16,9]{1,0:T(8,128)S(1)} copy-done((f32[16,9]{1,0:T(8,128)S(1)}, f32[16,9]{1,0:T(8,128)}, u32[]{:S(2)}) %copy-start) | copy-done | bytes 600
  3.9 0.0 copy-done.1
  3.9 0.0 copy-done.2
  3.9 0.0 copy-done.3
  3.9 28.1 %shard_map.123 = f32[24,128]{1,0:T(8,128)S(1)} custom-call(s32[8]{0:T(128)S(1)} %copy-done.1, s32[48]{0:T(128)S(1)} %copy-done.2, f32[48]{0:T(128)S(1)} %copy-done.3, f32[16,9]{1,0:T(8,128)S(1)} %copy-done, bf16[2,2,3,3,2,16,128]{6,5,4,3,2,1,0:T(8,128)(2,1)S(1)} %pad_maximum_fusion.vectors, f32[2,2,3,16,128]{4,3,2,1,0:T(8,128)S(1)} %pad_maximum_fusion.1.fields), custom_call_target="tpu_custom_call" | custom-call | tf_op jit(solution)/shard_map/pallas_call | solution.py:385
  32.0 0.1 reshape.123
  32.1 0.0 copy-start.7
  32.1 0.1 reshape.124
  32.2 0.0 copy-start.8
  32.2 0.6 %fusion.2 = f32[1,1152]{1,0:T(1,128)} fusion(f32[1,1152]{1,0:T(1,128)S(1)} %reshape.123, f32[1,9216]{1,0:T(1,128)S(1)} %copy-done.4, s32[]{:T(128)S(6)} %select_n.17), kind=kLoop, calls=%fused_computation.18 | loop fusion | flops 6912 | bytes 13828 | tf_op jit(solution)/shard_map/add | solution.py:418
  32.8 0.6 %multiply_subtract_fusion = f32[1,1152]{1,0:T(1,128)} fusion(f32[1,1152]{1,0:T(1,128)S(1)} %reshape.124, f32[1,9216]{1,0:T(1,128)S(1)} %copy-done.5, s32[]{:T(128)S(6)} %select_n.17), kind=kLoop, calls=%fused_computation.17 | loop fusion | flops 2304 | bytes 13828 | tf_op jit(solution)/shard_map/sub | solution.py:419
  33.4 0.0 copy-done.7
  33.4 0.0 copy-done.8
  (8 shorter events, 0.1 us)
Async XLA Ops:
  1.9 0.8 %copy-start.6 = (s32[1,9216]{1,0:T(1,128)S(1)}, s32[1,9216]{1,0:T(1,128)}, u32[]{:S(2)}) copy-start(s32[1,9216]{1,0:T(1,128)} %param.14) | copy-start | bytes 110596
  1.9 0.8 %copy-start.9 = (f32[32]{0:T(128)S(1)}, f32[32]{0:T(128)}, u32[]{:S(2)}) copy-start(f32[32]{0:T(128)} %param.15) | copy-start | bytes 388
  1.9 1.0 %copy-start.4 = (f32[1,9216]{1,0:T(1,128)S(1)}, f32[1,9216]{1,0:T(1,128)}, u32[]{:S(2)}) copy-start(f32[1,9216]{1,0:T(1,128)} %param.16) | copy-start | bytes 110596
  1.9 1.0 %copy-start.5 = (f32[1,9216]{1,0:T(1,128)S(1)}, f32[1,9216]{1,0:T(1,128)}, u32[]{:S(2)}) copy-start(f32[1,9216]{1,0:T(1,128)} %param.17) | copy-start | bytes 110596
  3.2 0.7 %copy-start = (f32[16,9]{1,0:T(8,128)S(1)}, f32[16,9]{1,0:T(8,128)}, u32[]{:S(2)}) copy-start(f32[16,9]{1,0:T(8,128)} %coef.1) | copy-start | bytes 1732
  3.2 0.7 %copy-start.1 = (s32[8]{0:T(128)S(1)}, s32[8]{0:T(128)}, u32[]{:S(2)}) copy-start(s32[8]{0:T(128)} %counts.1) | copy-start | bytes 100
  3.2 0.7 %copy-start.2 = (s32[48]{0:T(128)S(1)}, s32[48]{0:T(128)}, u32[]{:S(2)}) copy-start(s32[48]{0:T(128)} %slot_slice.1) | copy-start | bytes 580
  3.2 0.7 %copy-start.3 = (f32[48]{0:T(128)S(1)}, f32[48]{0:T(128)}, u32[]{:S(2)}) copy-start(f32[48]{0:T(128)} %occupation.1) | copy-start | bytes 580
  32.1 1.3 %copy-start.7 = (f32[1,1152]{1,0:T(1,128)}, f32[1,1152]{1,0:T(1,128)S(1)}, u32[]{:S(2)}) copy-start(f32[1,1152]{1,0:T(1,128)S(1)} %reshape.123) | copy-start | bytes 13828
  32.2 1.3 %copy-start.8 = (f32[1,1152]{1,0:T(1,128)}, f32[1,1152]{1,0:T(1,128)S(1)}, u32[]{:S(2)}) copy-start(f32[1,1152]{1,0:T(1,128)S(1)} %reshape.124) | copy-start | bytes 13828

commit v2 on v1

v2 whole, which is shorter than its diff:
```python
import functools

import jax
import jax.numpy as jnp
from jax import lax
from jax.experimental import pallas as pl
from jax.experimental.pallas import tpu as pltpu
from jax.sharding import PartitionSpec as P

NX = 96
DEGREE = 8
LANES = 128
PACK = 4
FLAT = 3
TILE = 16
SUBLANES = 8

spectral_scale = 8.5
beta_coef = 0.6
chem_level = 1.0
coupling = 1.0
density_floor = 0.05

MESH = pl.DeviceIdType.MESH


def round_up(value, step):
    return -(-value // step) * step


def plan(n_cuts, n_slab, cap, flat):
    groups = 2 if cap % 2 == 0 and n_slab % 2 == 0 else 1
    pieces = n_slab // groups
    total = flat // (NX * PACK)
    core = total // pieces
    halo = -(-DEGREE // PACK)
    width = min(round_up(core + halo, TILE), total)
    windows = (total - width) // SUBLANES + 1
    for piece in range(pieces):
        low, high = max(piece * core - halo, 0), min((piece + 1) * core + halo, total)
        start = SUBLANES * min(low // SUBLANES, windows - 1)
        assert start <= low and high <= start + width
    return groups, pieces, core, width, windows


def for_planes(count, body):
    chunk = 4 if count % 4 == 0 else 1
    if count == chunk:
        for z in range(chunk):
            body(z)
        return

    def some(i, carry):
        for z in range(chunk):
            body(i * chunk + z)
        return carry

    lax.fori_loop(0, count // chunk, some, 0)


def to_rows(flat_rows, lane):
    p0, p1, p2 = flat_rows
    r0, r1 = pltpu.roll(p0, 32, 1), pltpu.roll(p1, 32, 1)
    s1, s2 = pltpu.roll(p1, 64, 1), pltpu.roll(p2, 64, 1)
    rows = [
        p0,
        jnp.where(lane < 32, r0, r1),
        jnp.where(lane < 64, s1, s2),
        pltpu.roll(p2, 96, 1),
    ]
    return [jnp.where(lane < NX, row, 0.0) for row in rows]


def kernel(
    dims,
    counts_in,
    slot_slice_in,
    occupation_in,
    coef_in,
    table_in,
    index_in,
    mean_in,
    pairing_in,
    vectors,
    out,
    counts,
    slot_slice,
    occupation,
    coef,
    table,
    index_here,
    mean_here,
    fields,
    got_q,
    got_f,
    q_rows,
    ab,
    even,
    odd,
    dens,
    sibling,
    parts,
    landed,
    load_sem,
    q_send,
    q_recv,
    f_send,
    f_recv,
    s_send,
    s_recv,
    p_send,
    p_recv,
):
    n_cuts, nz, groups, pieces, core, width, windows, per_group, share_rows = dims
    cut, slab = lax.axis_index("cuts"), lax.axis_index("slab")
    near = n_cuts // pieces
    turn = max(near // 2, 1)
    home = cut // near
    cap = per_group * groups
    kept = nz // groups
    halo = -(-DEGREE // PACK)

    def piece_of(s):
        return (s // groups + cut // turn) % pieces

    def window_of(p):
        low = jnp.maximum(p * core - halo, 0)
        return jnp.minimum(low // SUBLANES, windows - 1)

    piece, group = piece_of(slab), slab % groups
    keeps_own = (home == piece).astype(jnp.int32)

    loads = [
        pltpu.make_async_copy(src, dst, load_sem.at[i])
        for i, (src, dst) in enumerate(
            [
                (index_in, index_here),
                (table_in, table),
                (mean_in, mean_here),
                (pairing_in, fields.at[1]),
                (counts_in, counts),
                (slot_slice_in, slot_slice),
                (occupation_in, occupation),
                (coef_in, coef),
            ]
        )
    ]
    for load in loads:
        load.start()

    others = [(slab + o) % nz for o in range(1, nz)]
    barrier = pltpu.get_barrier_semaphore()
    for to in others:
        pl.semaphore_signal(barrier, inc=1, device_id=(cut, to), device_id_type=MESH)

    def source_slab(c):
        return (home + pieces * n_cuts - c // turn) % pieces * groups + group

    for o in range(n_cuts):
        c = (cut + o) % n_cuts
        s = source_slab(c)

        def greet(c=c, s=s):
            pl.semaphore_signal(barrier, inc=1, device_id=(c, s), device_id_type=MESH)

        if o:
            greet()
        else:
            pl.when(s != slab)(greet)

    for load in loads[:4]:
        load.wait()
    hits = index_here[...]
    trap = jnp.zeros(hits.shape, jnp.float32)
    for level in range(table.shape[0]):
        trap = jnp.where(hits == level, table[level], trap)
    fields[0] = (2.0 / spectral_scale) * (3.0 + (trap + mean_here[...]))
    fields[1] = (2.0 / spectral_scale) * fields[1]

    pl.semaphore_wait(barrier, nz - 1 + near * kept - keeps_own)

    def field_copy(to):
        start = pl.multiple_of(window_of(piece_of(to)) * (SUBLANES * FLAT), SUBLANES)
        return pltpu.make_async_remote_copy(
            src_ref=fields.at[:, pl.ds(start, width * FLAT)],
            dst_ref=got_f.at[slab],
            send_sem=f_send.at[to],
            recv_sem=f_recv.at[slab],
            device_id=(cut, to),
            device_id_type=MESH,
        )

    def vector_copy(to, slot):
        return pltpu.make_async_remote_copy(
            src_ref=vectors.at[window_of(piece_of(to)), to % groups, slot],
            dst_ref=got_q.at[slot, slab],
            send_sem=q_send.at[slot, to],
            recv_sem=q_recv.at[slot, slab],
            device_id=(cut, to),
            device_id_type=MESH,
        )

    window = window_of(piece)
    for to in others:
        field_copy(to).start()
    for to in others:
        vector_copy(to, 0).start()
    own_start = pl.multiple_of(window * (SUBLANES * FLAT), SUBLANES)
    own_f = pltpu.make_async_copy(
        fields.at[:, pl.ds(own_start, width * FLAT)], got_f.at[slab], f_recv.at[slab]
    )
    own_f.start()

    def own_q(slot):
        return pltpu.make_async_copy(
            vectors.at[window, group, slot], got_q.at[slot, slab], q_recv.at[slot, slab]
        )

    own_q(0).start()
    for slot in range(1, per_group):
        for to in others:
            vector_copy(to, slot).start()
        own_q(slot).start()
    for load in loads[4:]:
        load.wait()

    lane = lax.broadcasted_iota(jnp.int32, (width, LANES), 1)
    line = lax.broadcasted_iota(jnp.int32, (width, LANES), 0)
    not_first, not_last = line > 0, line < width - 1
    hop = jnp.where(lane < NX, -1.0 / spectral_scale, 0.0).astype(jnp.float32)

    blank = jnp.zeros((2, PACK, width, LANES), jnp.float32)
    for buffer in (even, odd):
        buffer[:, 0] = blank
        buffer[:, nz + 1] = blank
    dens[...] = jnp.zeros(dens.shape, jnp.float32)

    def wait_fields(src):
        pltpu.make_async_remote_copy(
            src_ref=fields.at[:, pl.ds(own_start, width * FLAT)],
            dst_ref=got_f.at[src],
            send_sem=f_send.at[src],
            recv_sem=f_recv.at[src],
            device_id=(cut, src),
            device_id_type=MESH,
        ).wait_recv()

    own_f.wait()
    for src in others:
        wait_fields(src)

    def unpack_fields(z):
        for which in range(2):
            rows = to_rows(
                [got_f[z, which, pl.ds(j, width, stride=FLAT)] for j in range(FLAT)], lane
            )
            for i in range(PACK):
                ab[which, z, i] = rows[i]

    for_planes(nz, unpack_fields)

    def beside(ref, part, z):
        rows = [ref[part, z + 1, i] for i in range(PACK)]
        above = jnp.where(not_first, pltpu.roll(rows[-1], 1, 0), 0.0)
        below = jnp.where(not_last, pltpu.roll(rows[0], width - 1, 0), 0.0)
        padded = [above] + rows + [below]
        sums = []
        for i in range(PACK):
            around = pltpu.roll(rows[i], 1, 1) + pltpu.roll(rows[i], LANES - 1, 1)
            around = around + (padded[i] + padded[i + 2])
            around = around + (ref[part, z, i] + ref[part, z + 2, i])
            sums.append(hop * around)
        return rows, sums

    def twice_operator(ref, z):
        u, near_u = beside(ref, 0, z)
        v, near_v = beside(ref, 1, z)
        results = []
        for i in range(PACK):
            a, b = ab[0, z, i], ab[1, z, i]
            results.append((a * u[i] + b * v[i] + near_u[i], b * u[i] - a * v[i] - near_v[i]))
        return results

    def clenshaw(now, then, scale, first=False):
        def plane(z):
            for i, pair in enumerate(twice_operator(now, z)):
                for part in range(2):
                    value = scale * q_rows[part, z, i] + pair[part]
                    if not first:
                        value = value - then[part, z + 1, i]
                    then[part, z + 1, i] = value

        for_planes(nz, plane)

    def one_slot(slot, carry):
        own_q(slot).wait()
        for src in others:
            pltpu.make_async_remote_copy(
                src_ref=vectors.at[window, group, slot],
                dst_ref=got_q.at[slot, src],
                send_sem=q_send.at[slot, src],
                recv_sem=q_recv.at[slot, src],
                device_id=(cut, src),
                device_id_type=MESH,
            ).wait_recv()
        index = group * per_group + slot
        number = cut * cap + index
        level = slot_slice[number]
        weight = jnp.where(index < counts[cut], occupation[number], 0.0)
        last = coef[level, DEGREE]

        def unpack(z):
            for part in range(2):
                flat = [got_q[slot, z, j, part].astype(jnp.float32) for j in range(FLAT)]
                rows = to_rows(flat, lane)
                for i in range(PACK):
                    q_rows[part, z, i] = rows[i]
                    even[part, z + 1, i] = last * rows[i]

        for_planes(nz, unpack)
        clenshaw(even, odd, coef[level, DEGREE - 1], first=True)

        def two_steps(k, inner):
            order = DEGREE - 2 - 2 * k
            clenshaw(odd, even, coef[level, order])
            clenshaw(even, odd, coef[level, order - 1])
            return inner

        lax.fori_loop(0, (DEGREE - 2) // 2, two_steps, 0)
        base = coef[level, 0]

        def finish(z):
            for i, pair in enumerate(twice_operator(odd, z)):
                f = [
                    base * q_rows[part, z, i] + 0.5 * pair[part] - even[part, z + 1, i]
                    for part in range(2)
                ]
                heavy = weight * f[1]
                dens[z, 0, i] += heavy * f[1]
                dens[z, 1, i] += heavy * f[0]

        for_planes(nz, finish)
        return carry

    lax.fori_loop(0, per_group, one_slot, 0)

    inside = piece * core - window * SUBLANES
    mate = slab + 1 - 2 * group

    def sibling_copy(k):
        return pltpu.make_async_remote_copy(
            src_ref=dens.at[groups * k + 1 - group],
            dst_ref=sibling.at[k],
            send_sem=s_send.at[k],
            recv_sem=s_recv.at[k],
            device_id=(cut, mate),
            device_id_type=MESH,
        )

    def part_copy(c, k):
        return pltpu.make_async_remote_copy(
            src_ref=parts.at[c, k],
            dst_ref=landed.at[cut],
            send_sem=p_send.at[c, k],
            recv_sem=p_recv.at[cut],
            device_id=(piece * near + c, groups * k + group),
            device_id_type=MESH,
        )

    def elsewhere(c, k):
        return jnp.logical_or(piece * near + c != cut, groups * k + group != slab)

    def pack(c, k):
        z = groups * k + group
        if share_rows % PACK == 0:
            step = share_rows // PACK
            spans = [(i, i, c * step, step) for i in range(PACK)]
        else:
            rows = [(r, c * share_rows + r) for r in range(share_rows)]
            spans = [(r, y % PACK, y // PACK, 1) for r, y in rows]
        for which in range(2):
            for r, i, g, n in spans:
                value = dens[z, which, i, pl.ds(inside + g, n)]
                if groups > 1:
                    value = value + sibling[k, which, i, pl.ds(inside + g, n)]
                if n == 1:
                    parts[c, k, pl.ds(which * share_rows + r, 1)] = value
                else:
                    parts[c, k, pl.ds(which * share_rows + r, n, stride=PACK)] = value

    if groups > 1:
        for k in range(kept):
            sibling_copy(k).start()
    for k in range(kept):
        if groups > 1:
            sibling_copy(k).wait_recv()
        for c in range(near):
            pack(c, k)
            pl.when(elsewhere(c, k))(part_copy(c, k).start)

    @pl.when(home == piece)
    def _():
        landed[cut] = parts[cut % near, slab // groups]

    for o in range(n_cuts):
        c = (cut + o) % n_cuts

        def arrive(c=c):
            pltpu.make_async_remote_copy(
                src_ref=parts.at[0, 0],
                dst_ref=landed.at[c],
                send_sem=p_send.at[0, 0],
                recv_sem=p_recv.at[c],
                device_id=(c, source_slab(c)),
                device_id_type=MESH,
            ).wait_recv()

        if o:
            arrive()
        else:
            pl.when(source_slab(c) != slab)(arrive)
    total = landed[0]
    for source in range(1, n_cuts):
        total = total + landed[source]
    out[...] = total

    for to in others:
        field_copy(to).wait_send()
        for slot in range(per_group):
            vector_copy(to, slot).wait_send()
    for k in range(kept):
        if groups > 1:
            sibling_copy(k).wait_send()
        for c in range(near):
            pl.when(elsewhere(c, k))(part_copy(c, k).wait_send)


def body(
    quasi, counts, slot_slice, occupation, filter_coef, trap_index, trap_table, mean_field, pairing
):
    n_cuts, nz = lax.axis_size("cuts"), lax.axis_size("slab")
    cut = lax.axis_index("cuts")
    cap, flat = quasi.shape[1], quasi.shape[3]
    share = flat // n_cuts
    share_rows = share // NX
    groups, pieces, core, width, windows = plan(n_cuts, nz, cap, flat)
    per_group = cap // groups
    n_groups = flat // (NX * PACK)

    q = quasi.reshape(2, groups, per_group, n_groups, FLAT, LANES)
    q = q.transpose(1, 2, 4, 0, 3, 5)
    starts = [SUBLANES * w for w in range(windows)]
    vectors = jnp.stack([q[:, :, :, :, s : s + width] for s in starts])

    rows = round_up(2 * share_rows, SUBLANES)
    near = n_cuts // pieces
    kept = nz // groups
    dims = (n_cuts, nz, groups, pieces, core, width, windows, per_group, share_rows)
    f32, i32 = jnp.float32, jnp.int32
    tall = (flat // LANES, LANES)
    slots = slot_slice.shape[0]
    sums = pl.pallas_call(
        functools.partial(kernel, dims),
        out_shape=jax.ShapeDtypeStruct((rows, LANES), f32),
        in_specs=[pl.BlockSpec(memory_space=pltpu.HBM)] * 8
        + [pl.BlockSpec(memory_space=pl.ANY)],
        out_specs=pl.BlockSpec(memory_space=pltpu.VMEM),
        scratch_shapes=[
            pltpu.SMEM((n_cuts,), i32),
            pltpu.SMEM((slots,), i32),
            pltpu.SMEM((slots,), f32),
            pltpu.SMEM(filter_coef.shape, f32),
            pltpu.SMEM(trap_table.shape, f32),
            pltpu.VMEM(tall, i32),
            pltpu.VMEM(tall, f32),
            pltpu.VMEM((2, *tall), f32),
            pltpu.VMEM((per_group, nz, FLAT, 2, width, LANES), jnp.bfloat16),
            pltpu.VMEM((nz, 2, FLAT * width, LANES), f32),
            pltpu.VMEM((2, nz, PACK, width, LANES), f32),
            pltpu.VMEM((2, nz, PACK, width, LANES), f32),
            pltpu.VMEM((2, nz + 2, PACK, width, LANES), f32),
            pltpu.VMEM((2, nz + 2, PACK, width, LANES), f32),
            pltpu.VMEM((nz, 2, PACK, width, LANES), f32),
            pltpu.VMEM((kept, 2, PACK, width, LANES), f32),
            pltpu.VMEM((near, kept, rows, LANES), f32),
            pltpu.VMEM((n_cuts, rows, LANES), f32),
            pltpu.SemaphoreType.DMA((8,)),
            pltpu.SemaphoreType.DMA((per_group, nz)),
            pltpu.SemaphoreType.DMA((per_group, nz)),
            pltpu.SemaphoreType.DMA((nz,)),
            pltpu.SemaphoreType.DMA((nz,)),
            pltpu.SemaphoreType.DMA((kept,)),
            pltpu.SemaphoreType.DMA((kept,)),
            pltpu.SemaphoreType.DMA((near, kept)),
            pltpu.SemaphoreType.DMA((n_cuts,)),
        ],
        compiler_params=pltpu.CompilerParams(
            collective_id=0, has_side_effects=True, vmem_limit_bytes=48 * 1024 * 1024
        ),
    )(
        counts,
        slot_slice,
        occupation,
        filter_coef,
        trap_table,
        trap_index.reshape(tall),
        mean_field.reshape(tall),
        pairing.reshape(tall),
        vectors,
    )

    flat_sums = sums[: 2 * share_rows, :NX].reshape(2, share)
    normal_density, anomalous_density = flat_sums[:1], flat_sums[1:]
    mean_local = lax.dynamic_slice_in_dim(mean_field, cut * share, share, 1)
    pairing_local = lax.dynamic_slice_in_dim(pairing, cut * share, share, 1)
    cube_root = jnp.cbrt(normal_density + density_floor)
    new_mean_field = 0.5 * mean_local + 0.5 * (beta_coef * cube_root * cube_root - chem_level)
    new_pairing = 0.5 * pairing_local - coupling * anomalous_density
    return (normal_density, anomalous_density, new_mean_field, new_pairing)


def solution(mesh):
    return jax.shard_map(
        body,
        mesh=mesh,
        in_specs=(
            P(None, "cuts", "slab", None),
            P(),
            P(),
            P(),
            P(),
            P("slab", None),
            P(),
            P("slab", None),
            P("slab", None),
        ),
        out_specs=(P("slab", "cuts"), P("slab", "cuts"), P("slab", "cuts"), P("slab", "cuts")),
        check_vma=False,
    )
```

time: 33.7 us -> 26.3 us (0.78)
  Pallas kernels: 28.1 us -> 21.9 us
  other arithmetic: 1.73 us -> 0.68 us
    pallas_call x1, Pallas kernels: 28.1 us -> 21.9 us  [body(): pl.pallas_call(functools.partial(kernel, dims), out_shape=jax.ShapeDtypeS...]
    add x2 -> x0, other arithmetic: 0.65 us -> none  [the longest x1 0.65 us: body(): 0.5 * mean_local + 0.5 * (beta_coef * cube_root * cube_root - chem_level)]
where the time goes in v2:
time: 26.3 us; the launch traced here: 26 us
  Pallas kernels  21.9 us (83%)
  local copies, waits for them, and re-layouts  2.68 us (10%)
  between operations  0.76 us (3%)
  other arithmetic  0.68 us (3%)
    pallas_call x1, Pallas kernels, body(): pl.pallas_call(functools.partial(kernel, dims), out_shape=jax.ShapeDtypeS...  21.9 us
    unnamed x20, local copies, waits for them, and re-layouts  1.31 us
    reshape x2, local copies, waits for them, and re-layouts, body(): q = quasi.reshape(2, groups, per_group, n_groups, FLAT, LANES)  1.16 us
    sub x1, other arithmetic, body(): new_pairing = 0.5 * pairing_local - coupling * anomalous_density  0.65 us

profile of v2, /device:TPU:0, one launch (start us, length us, event | category | flops | bytes accessed | tf_op | source)
XLA Modules:
  0.0 26.0 jit_solution(12167712511155580184)
XLA Ops:
  0.6 1.1 %reshape.54 = bf16[2,2,3,24,3,128]{5,4,3,0,2,1:T(4,128)(2,1)S(1)} reshape(bf16[2,6,1,9216]{3,0,2,1:T(2,128)(2,1)} %param.9) | data formatting | bytes 442368 | tf_op jit(solution)/shard_map/reshape | solution.py:450
  1.9 0.0 copy-start
  1.9 0.0 copy-start.1
  1.9 0.0 copy-start.2
  1.9 0.0 copy-start.3
  1.9 0.0 copy-start.4
  1.9 0.0 copy-start.5
  1.9 0.0 copy-start.6
  1.9 0.0 copy-start.7
  2.0 0.6 %copy-done = f32[1,9216]{1,0:T(1,128)S(1)} copy-done((f32[1,9216]{1,0:T(1,128)S(1)}, f32[1,9216]{1,0:T(1,128)}, u32[]{:S(2)}) %copy-start) | copy-done | bytes 36888
  2.6 0.0 copy-done.1
  2.6 0.0 copy-done.2
  2.7 0.0 copy-done.3
  2.7 0.0 copy-done.4
  2.7 0.0 copy-done.5
  2.7 0.0 copy-done.6
  2.7 0.0 copy-done.7
  2.7 21.9 %shard_map.120 = f32[24,128]{1,0:T(8,128)S(1)} custom-call(s32[8]{0:T(128)S(1)} %copy-done.4, s32[48]{0:T(128)S(1)} %copy-done.5, f32[48]{0:T(128)S(1)} %copy-done.6, f32[16,9]{1,0:T(8,128)S(1)} %copy-done.3, f32[32]{0:T(128)S(1)} %copy-done.7, s32[72,128]{1,0:T(8,128)S(1)} %bitcast.14, f32[72,128]{1,0:T(8,128)S(1)} %bitcast.12, f32[72,128]{1,0:T(8,128)S(1)} %bitcast.13, ...), custom_call_target="tpu_custom_call" | custom-call | tf_op jit(solution)/shard_map/pallas_call | solution.py:462
  24.6 0.1 slice.24
  24.7 0.0 copy-start.8
  24.7 0.1 slice.26
  24.8 0.0 copy-start.9
  24.8 0.5 %copy-done.8 = f32[1,1152]{1,0:T(1,128)} copy-done((f32[1,1152]{1,0:T(1,128)}, f32[1,1152]{1,0:T(1,128)S(1)}, u32[]{:S(2)}) %copy-start.8) | copy-done | bytes 4632
  25.3 0.1 copy-done.9
  25.4 0.6 %multiply_subtract_fusion = (f32[1,1152]{1,0:T(1,128)}, f32[1,1152]{1,0:T(1,128)}) fusion(f32[1,1152]{1,0:T(1,128)S(1)} %slice.26, f32[1,9216]{1,0:T(1,128)S(1)} %copy-done.1, s32[]{:T(128)S(6)} %select_n.4, f32[1,1152]{1,0:T(1,128)S(1)} %slice.24, f32[1,9216]{1,0:T(1,128)S(1)} %copy-done), kind=kLoop, calls=%fused_computation.7 | loop fusion | flops 9216 | bytes 27652 | tf_op jit(solution)/shard_map/sub | solution.py:518
  (4 shorter events, 0.1 us)
Async XLA Ops:
  1.9 0.8 %copy-start = (f32[1,9216]{1,0:T(1,128)S(1)}, f32[1,9216]{1,0:T(1,128)}, u32[]{:S(2)}) copy-start(f32[1,9216]{1,0:T(1,128)} %param.16) | copy-start | bytes 110596
  1.9 0.8 %copy-start.1 = (f32[1,9216]{1,0:T(1,128)S(1)}, f32[1,9216]{1,0:T(1,128)}, u32[]{:S(2)}) copy-start(f32[1,9216]{1,0:T(1,128)} %param.17) | copy-start | bytes 110596
  1.9 0.8 %copy-start.2 = (s32[1,9216]{1,0:T(1,128)S(1)}, s32[1,9216]{1,0:T(1,128)}, u32[]{:S(2)}) copy-start(s32[1,9216]{1,0:T(1,128)} %param.14) | copy-start | bytes 110596
  1.9 0.8 %copy-start.3 = (f32[16,9]{1,0:T(8,128)S(1)}, f32[16,9]{1,0:T(8,128)}, u32[]{:S(2)}) copy-start(f32[16,9]{1,0:T(8,128)} %coef_in.1) | copy-start | bytes 1732
  1.9 0.8 %copy-start.4 = (s32[8]{0:T(128)S(1)}, s32[8]{0:T(128)}, u32[]{:S(2)}) copy-start(s32[8]{0:T(128)} %counts_in.1) | copy-start | bytes 100
  1.9 0.8 %copy-start.5 = (s32[48]{0:T(128)S(1)}, s32[48]{0:T(128)}, u32[]{:S(2)}) copy-start(s32[48]{0:T(128)} %slot_slice_in.1) | copy-start | bytes 580
  1.9 0.7 %copy-start.6 = (f32[48]{0:T(128)S(1)}, f32[48]{0:T(128)}, u32[]{:S(2)}) copy-start(f32[48]{0:T(128)} %occupation_in.1) | copy-start | bytes 580
  1.9 0.7 %copy-start.7 = (f32[32]{0:T(128)S(1)}, f32[32]{0:T(128)}, u32[]{:S(2)}) copy-start(f32[32]{0:T(128)} %table_in.1) | copy-start | bytes 388
  24.7 0.6 %copy-start.8 = (f32[1,1152]{1,0:T(1,128)}, f32[1,1152]{1,0:T(1,128)S(1)}, u32[]{:S(2)}) copy-start(f32[1,1152]{1,0:T(1,128)S(1)} %slice.24) | copy-start | bytes 13828
  24.8 0.6 %copy-start.9 = (f32[1,1152]{1,0:T(1,128)}, f32[1,1152]{1,0:T(1,128)S(1)}, u32[]{:S(2)}) copy-start(f32[1,1152]{1,0:T(1,128)S(1)} %slice.26) | copy-start | bytes 13828

commit v3 on v2

--- a/solution.py
+++ b/solution.py
@@ -14,6 +14,7 @@
 FLAT = 3
 TILE = 16
 SUBLANES = 8
+VMEM_BYTES = 65000 * 1024
 
 spectral_scale = 8.5
 beta_coef = 0.6
@@ -93,6 +94,7 @@
     fields,
     got_q,
     got_f,
+    wide,
     q_rows,
     ab,
     even,
@@ -130,6 +132,26 @@
     piece, group = piece_of(slab), slab % groups
     keeps_own = (home == piece).astype(jnp.int32)
 
+    others = [(slab + o) % nz for o in range(1, nz)]
+    barrier = pltpu.get_barrier_semaphore()
+    for to in others:
+        pl.semaphore_signal(barrier, inc=1, device_id=(cut, to), device_id_type=MESH)
+
+    def source_slab(c):
+        return (home + pieces * n_cuts - c // turn) % pieces * groups + group
+
+    for o in range(n_cuts):
+        c = (cut + o) % n_cuts
+        s = source_slab(c)
+
+        def greet(c=c, s=s):
+            pl.semaphore_signal(barrier, inc=1, device_id=(c, s), device_id_type=MESH)
+
+        if o:
+            greet()
+        else:
+            pl.when(s != slab)(greet)
+
     loads = [
         pltpu.make_async_copy(src, dst, load_sem.at[i])
         for i, (src, dst) in enumerate(
@@ -148,26 +170,6 @@
     for load in loads:
         load.start()
 
-    others = [(slab + o) % nz for o in range(1, nz)]
-    barrier = pltpu.get_barrier_semaphore()
-    for to in others:
-        pl.semaphore_signal(barrier, inc=1, device_id=(cut, to), device_id_type=MESH)
-
-    def source_slab(c):
-        return (home + pieces * n_cuts - c // turn) % pieces * groups + group
-
-    for o in range(n_cuts):
-        c = (cut + o) % n_cuts
-        s = source_slab(c)
-
-        def greet(c=c, s=s):
-            pl.semaphore_signal(barrier, inc=1, device_id=(c, s), device_id_type=MESH)
-
-        if o:
-            greet()
-        else:
-            pl.when(s != slab)(greet)
-
     for load in loads[:4]:
         load.wait()
     hits = index_here[...]
@@ -178,6 +180,18 @@
     fields[1] = (2.0 / spectral_scale) * fields[1]
 
     pl.semaphore_wait(barrier, nz - 1 + near * kept - keeps_own)
+
+    mate = slab + 1 - 2 * group
+
+    def passed_on(src):
+        return pltpu.make_async_remote_copy(
+            src_ref=got_f.at[src],
+            dst_ref=got_f.at[src],
+            send_sem=f_send.at[nz + src],
+            recv_sem=f_recv.at[src],
+            device_id=(cut, mate),
+            device_id_type=MESH,
+        )
 
     def field_copy(to):
         start = pl.multiple_of(window_of(piece_of(to)) * (SUBLANES * FLAT), SUBLANES)
@@ -192,7 +206,9 @@
 
     def vector_copy(to, slot):
         return pltpu.make_async_remote_copy(
-            src_ref=vectors.at[window_of(piece_of(to)), to % groups, slot],
+            src_ref=vectors.at[
+                to % groups * per_group + slot, pl.ds(window_of(piece_of(to)) * (SUBLANES * FLAT), width * FLAT)
+            ],
             dst_ref=got_q.at[slot, slab],
             send_sem=q_send.at[slot, to],
             recv_sem=q_recv.at[slot, slab],
@@ -201,7 +217,9 @@
         )
 
     window = window_of(piece)
-    for to in others:
+    alike = [(slab + o) % nz for o in range(groups, nz, groups)]
+    direct = alike + ([mate] if groups > 1 else [])
+    for to in direct:
         field_copy(to).start()
     for to in others:
         vector_copy(to, 0).start()
@@ -213,7 +231,9 @@
 
     def own_q(slot):
         return pltpu.make_async_copy(
-            vectors.at[window, group, slot], got_q.at[slot, slab], q_recv.at[slot, slab]
+            vectors.at[group * per_group + slot, pl.ds(own_start, width * FLAT)],
+            got_q.at[slot, slab],
+            q_recv.at[slot, slab],
         )
 
     own_q(0).start()
@@ -245,9 +265,15 @@
             device_id_type=MESH,
         ).wait_recv()
 
+    for src in alike:
+        wait_fields(src)
+        if groups > 1:
+            passed_on(src).start()
     own_f.wait()
-    for src in others:
-        wait_fields(src)
+    if groups > 1:
+        wait_fields(mate)
+        for src in alike:
+            wait_fields(src + 1 - 2 * group)
 
     def unpack_fields(z):
         for which in range(2):
@@ -292,11 +318,21 @@
 
         for_planes(nz, plane)
 
+    def sibling_copy(k):
+        return pltpu.make_async_remote_copy(
+            src_ref=dens.at[groups * k + 1 - group],
+            dst_ref=sibling.at[k],
+            send_sem=s_send.at[k],
+            recv_sem=s_recv.at[k],
+            device_id=(cut, mate),
+            device_id_type=MESH,
+        )
+
     def one_slot(slot, carry):
         own_q(slot).wait()
         for src in others:
             pltpu.make_async_remote_copy(
-                src_ref=vectors.at[window, group, slot],
+                src_ref=vectors.at[slot, pl.ds(own_start, width * FLAT)],
                 dst_ref=got_q.at[slot, src],
                 send_sem=q_send.at[slot, src],
                 recv_sem=q_recv.at[slot, src],
@@ -310,8 +346,12 @@
         last = coef[level, DEGREE]
 
         def unpack(z):
+            for r in range(width * FLAT):
+                wide[z, pl.ds(2 * r, 2)] = got_q[slot, z, r].astype(jnp.float32)
             for part in range(2):
-                flat = [got_q[slot, z, j, part].astype(jnp.float32) for j in range(FLAT)]
+                flat = [
+                    wide[z, pl.ds(2 * j + part, width, stride=2 * FLAT)] for j in range(FLAT)
+                ]
                 rows = to_rows(flat, lane)
                 for i in range(PACK):
                     q_rows[part, z, i] = rows[i]
@@ -339,24 +379,19 @@
                 dens[z, 0, i] += heavy * f[1]
                 dens[z, 1, i] += heavy * f[0]
 
-        for_planes(nz, finish)
+        if groups == 1:
+            for_planes(nz, finish)
+            return carry
+        for k in range(kept):
+            finish(groups * k + 1 - group)
+            pl.when(slot == per_group - 1)(sibling_copy(k).start)
+        for k in range(kept):
+            finish(groups * k + group)
         return carry
 
     lax.fori_loop(0, per_group, one_slot, 0)
 
     inside = piece * core - window * SUBLANES
-    mate = slab + 1 - 2 * group
-
-    def sibling_copy(k):
-        return pltpu.make_async_remote_copy(
-            src_ref=dens.at[groups * k + 1 - group],
-            dst_ref=sibling.at[k],
-            send_sem=s_send.at[k],
-            recv_sem=s_recv.at[k],
-            device_id=(cut, mate),
-            device_id_type=MESH,
-        )
-
     def part_copy(c, k):
         return pltpu.make_async_remote_copy(
             src_ref=parts.at[c, k],
@@ -388,9 +423,6 @@
                 else:
                     parts[c, k, pl.ds(which * share_rows + r, n, stride=PACK)] = value
 
-    if groups > 1:
-        for k in range(kept):
-            sibling_copy(k).start()
     for k in range(kept):
         if groups > 1:
             sibling_copy(k).wait_recv()
@@ -424,8 +456,12 @@
         total = total + landed[source]
     out[...] = total
 
+    for to in direct:
+        field_copy(to).wait_send()
+    if groups > 1:
+        for src in alike:
+            passed_on(src).wait_send()
     for to in others:
-        field_copy(to).wait_send()
         for slot in range(per_group):
             vector_copy(to, slot).wait_send()
     for k in range(kept):
@@ -445,12 +481,7 @@
     share_rows = share // NX
     groups, pieces, core, width, windows = plan(n_cuts, nz, cap, flat)
     per_group = cap // groups
-    n_groups = flat // (NX * PACK)
-
-    q = quasi.reshape(2, groups, per_group, n_groups, FLAT, LANES)
-    q = q.transpose(1, 2, 4, 0, 3, 5)
-    starts = [SUBLANES * w for w in range(windows)]
-    vectors = jnp.stack([q[:, :, :, :, s : s + width] for s in starts])
+    vectors = quasi.reshape(2, cap, flat // LANES, LANES).transpose(1, 2, 0, 3)
 
     rows = round_up(2 * share_rows, SUBLANES)
     near = n_cuts // pieces
@@ -474,8 +505,9 @@
             pltpu.VMEM(tall, i32),
             pltpu.VMEM(tall, f32),
             pltpu.VMEM((2, *tall), f32),
-            pltpu.VMEM((per_group, nz, FLAT, 2, width, LANES), jnp.bfloat16),
+            pltpu.VMEM((per_group, nz, FLAT * width, 2, LANES), jnp.bfloat16),
             pltpu.VMEM((nz, 2, FLAT * width, LANES), f32),
+            pltpu.VMEM((nz, 2 * FLAT * width, LANES), f32),
             pltpu.VMEM((2, nz, PACK, width, LANES), f32),
             pltpu.VMEM((2, nz, PACK, width, LANES), f32),
             pltpu.VMEM((2, nz + 2, PACK, width, LANES), f32),
@@ -487,7 +519,7 @@
             pltpu.SemaphoreType.DMA((8,)),
             pltpu.SemaphoreType.DMA((per_group, nz)),
             pltpu.SemaphoreType.DMA((per_group, nz)),
-            pltpu.SemaphoreType.DMA((nz,)),
+            pltpu.SemaphoreType.DMA((2 * nz,)),
             pltpu.SemaphoreType.DMA((nz,)),
             pltpu.SemaphoreType.DMA((kept,)),
             pltpu.SemaphoreType.DMA((kept,)),
@@ -495,7 +527,7 @@
             pltpu.SemaphoreType.DMA((n_cuts,)),
         ],
         compiler_params=pltpu.CompilerParams(
-            collective_id=0, has_side_effects=True, vmem_limit_bytes=48 * 1024 * 1024
+            collective_id=0, has_side_effects=True, vmem_limit_bytes=VMEM_BYTES
         ),
     )(
         counts,

time: 26.3 us -> 25.8 us (0.981)
  local copies, waits for them, and re-layouts: 2.68 us -> 1.53 us
  other arithmetic: 0.68 us -> 1.35 us
    reshape x2 -> x0, local copies, waits for them, and re-layouts: 1.16 us -> none  [body(): q = quasi.reshape(2, groups, per_group, n_groups, FLAT, LANES)]
    slice x3, local copies, waits for them, and re-layouts: 0.16 us -> 0.94 us  [body(): normal_density, anomalous_density = (flat_sums[:1], flat_sums[1:])]
    unnamed x20 -> x4, local copies, waits for them, and re-layouts: 1.31 us -> 0.59 us
    sub x1, other arithmetic: 0.65 us -> 1.35 us  [body(): new_pairing = 0.5 * pairing_local - coupling * anomalous_density]
where the time goes in v3:
time: 25.8 us; the launch traced here: 25.5 us
  Pallas kernels  22 us (85%)
  local copies, waits for them, and re-layouts  1.53 us (6%)
  other arithmetic  1.35 us (5%)
  between operations  0.65 us (3%)
    pallas_call x1, Pallas kernels, body(): pl.pallas_call(functools.partial(kernel, dims), out_shape=jax.ShapeDtypeS...  22 us
    sub x1, other arithmetic, body(): new_pairing = 0.5 * pairing_local - coupling * anomalous_density  1.35 us
    slice x3, local copies, waits for them, and re-layouts, body(): normal_density, anomalous_density = (flat_sums[:1], flat_sums[1:])  0.94 us
    unnamed x4, local copies, waits for them, and re-layouts  0.59 us

profile of v3, /device:TPU:0, one launch (start us, length us, event | category | flops | bytes accessed | tf_op | source)
XLA Modules:
  0.0 25.5 jit_solution(2221761451600834485)
XLA Ops:
  0.6 22.0 %shard_map.120 = f32[24,128]{1,0:T(8,128)} custom-call(s32[8]{0:T(128)} %counts_in.1, s32[48]{0:T(128)} %slot_slice_in.1, f32[48]{0:T(128)} %occupation_in.1, f32[16,9]{1,0:T(8,128)} %coef_in.1, f32[32]{0:T(128)} %table_in.1, s32[72,128]{1,0:T(8,128)} %bitcast.9, f32[72,128]{1,0:T(8,128)} %bitcast.7, f32[72,128]{1,0:T(8,128)} %bitcast.8, ...), custom_call_target="tpu_custom_call" | custom-call | tf_op jit(solution)/shard_map/pallas_call | solution.py:493
  22.6 0.8 %fusion.3 = (f32[12,96]{1,0:T(8,128)S(1)}, f32[12,96]{1,0:T(8,128)S(1)}) fusion(f32[24,128]{1,0:T(8,128)} %shard_map.120), kind=kLoop, calls=%fused_computation.5 | loop fusion | bytes 18432 | tf_op jit(solution)/shard_map/slice | solution.py:545
  23.4 0.1 slice.16
  23.5 0.0 copy-start
  23.5 0.1 slice.18
  23.5 0.0 copy-start.1
  23.6 0.5 %copy-done = f32[1,1152]{1,0:T(1,128)} copy-done((f32[1,1152]{1,0:T(1,128)}, f32[1,1152]{1,0:T(1,128)S(1)}, u32[]{:S(2)}) %copy-start) | copy-done | bytes 4632
  24.1 0.1 copy-done.1
  24.1 1.4 %multiply_subtract_fusion = (f32[1,1152]{1,0:T(1,128)}, f32[1,1152]{1,0:T(1,128)}) fusion(f32[1,1152]{1,0:T(1,128)S(1)} %slice.18, f32[1,9216]{1,0:T(1,128)} %param.17, s32[]{:T(128)S(6)} %select_n.4, f32[1,1152]{1,0:T(1,128)S(1)} %slice.16, f32[1,9216]{1,0:T(1,128)} %param.16), kind=kLoop, calls=%fused_computation.3 | loop fusion | flops 9216 | bytes 27652 | tf_op jit(solution)/shard_map/sub | solution.py:550
Async XLA Ops:
  23.5 0.6 %copy-start = (f32[1,1152]{1,0:T(1,128)}, f32[1,1152]{1,0:T(1,128)S(1)}, u32[]{:S(2)}) copy-start(f32[1,1152]{1,0:T(1,128)S(1)} %slice.16) | copy-start | bytes 13828
  23.5 0.6 %copy-start.1 = (f32[1,1152]{1,0:T(1,128)}, f32[1,1152]{1,0:T(1,128)S(1)}, u32[]{:S(2)}) copy-start(f32[1,1152]{1,0:T(1,128)S(1)} %slice.18) | copy-start | bytes 13828

commit v4 on v3

--- a/solution.py
+++ b/solution.py
@@ -59,8 +59,9 @@
     lax.fori_loop(0, count // chunk, some, 0)
 
 
-def to_rows(flat_rows, lane):
+def to_rows(flat_rows):
     p0, p1, p2 = flat_rows
+    lane = lax.broadcasted_iota(jnp.int32, p0.shape, 1)
     r0, r1 = pltpu.roll(p0, 32, 1), pltpu.roll(p1, 32, 1)
     s1, s2 = pltpu.roll(p1, 64, 1), pltpu.roll(p2, 64, 1)
     rows = [
@@ -91,6 +92,8 @@
     table,
     index_here,
     mean_here,
+    pairing_here,
+    local_rows,
     fields,
     got_q,
     got_f,
@@ -137,21 +140,6 @@
     for to in others:
         pl.semaphore_signal(barrier, inc=1, device_id=(cut, to), device_id_type=MESH)
 
-    def source_slab(c):
-        return (home + pieces * n_cuts - c // turn) % pieces * groups + group
-
-    for o in range(n_cuts):
-        c = (cut + o) % n_cuts
-        s = source_slab(c)
-
-        def greet(c=c, s=s):
-            pl.semaphore_signal(barrier, inc=1, device_id=(c, s), device_id_type=MESH)
-
-        if o:
-            greet()
-        else:
-            pl.when(s != slab)(greet)
-
     loads = [
         pltpu.make_async_copy(src, dst, load_sem.at[i])
         for i, (src, dst) in enumerate(
@@ -159,7 +147,7 @@
                 (index_in, index_here),
                 (table_in, table),
                 (mean_in, mean_here),
-                (pairing_in, fields.at[1]),
+                (pairing_in, pairing_here),
                 (counts_in, counts),
                 (slot_slice_in, slot_slice),
                 (occupation_in, occupation),
@@ -169,6 +157,21 @@
     ]
     for load in loads:
         load.start()
+
+    def source_slab(c):
+        return (home + pieces * n_cuts - c // turn) % pieces * groups + group
+
+    for o in range(n_cuts):
+        c = (cut + o) % n_cuts
+        s = source_slab(c)
+
+        def greet(c=c, s=s):
+            pl.semaphore_signal(barrier, inc=1, device_id=(c, s), device_id_type=MESH)
+
+        if o:
+            greet()
+        else:
+            pl.when(s != slab)(greet)
 
     for load in loads[:4]:
         load.wait()
@@ -177,7 +180,7 @@
     for level in range(table.shape[0]):
         trap = jnp.where(hits == level, table[level], trap)
     fields[0] = (2.0 / spectral_scale) * (3.0 + (trap + mean_here[...]))
-    fields[1] = (2.0 / spectral_scale) * fields[1]
+    fields[1] = (2.0 / spectral_scale) * pairing_here[...]
 
     pl.semaphore_wait(barrier, nz - 1 + near * kept - keeps_own)
 
@@ -205,10 +208,9 @@
         )
 
     def vector_copy(to, slot):
+        start = window_of(piece_of(to)) * (SUBLANES * FLAT)
         return pltpu.make_async_remote_copy(
-            src_ref=vectors.at[
-                to % groups * per_group + slot, pl.ds(window_of(piece_of(to)) * (SUBLANES * FLAT), width * FLAT)
-            ],
+            src_ref=vectors.at[to % groups * per_group + slot, pl.ds(start, width * FLAT)],
             dst_ref=got_q.at[slot, slab],
             send_sem=q_send.at[slot, to],
             recv_sem=q_recv.at[slot, slab],
@@ -237,10 +239,6 @@
         )
 
     own_q(0).start()
-    for slot in range(1, per_group):
-        for to in others:
-            vector_copy(to, slot).start()
-        own_q(slot).start()
     for load in loads[4:]:
         load.wait()
 
@@ -254,6 +252,15 @@
         buffer[:, 0] = blank
         buffer[:, nz + 1] = blank
     dens[...] = jnp.zeros(dens.shape, jnp.float32)
+
+    for part, here in enumerate((mean_here, pairing_here)):
+        count = here.shape[0] // FLAT
+        rows = to_rows([here[pl.ds(j, count, stride=FLAT)] for j in range(FLAT)])
+        for i in range(PACK):
+            local_rows[part, i] = rows[i]
+        for r in range(share_rows):
+            y = cut * share_rows + r
+            out[part, pl.ds(2 * share_rows + r, 1)] = local_rows[part, y % PACK, pl.ds(y // PACK, 1)]
 
     def wait_fields(src):
         pltpu.make_async_remote_copy(
@@ -269,6 +276,10 @@
         wait_fields(src)
         if groups > 1:
             passed_on(src).start()
+    for slot in range(1, per_group):
+        for to in others:
+            vector_copy(to, slot).start()
+        own_q(slot).start()
     own_f.wait()
     if groups > 1:
         wait_fields(mate)
@@ -278,7 +289,7 @@
     def unpack_fields(z):
         for which in range(2):
             rows = to_rows(
-                [got_f[z, which, pl.ds(j, width, stride=FLAT)] for j in range(FLAT)], lane
+                [got_f[z, which, pl.ds(j, width, stride=FLAT)] for j in range(FLAT)]
             )
             for i in range(PACK):
                 ab[which, z, i] = rows[i]
@@ -352,7 +363,7 @@
                 flat = [
                     wide[z, pl.ds(2 * j + part, width, stride=2 * FLAT)] for j in range(FLAT)
                 ]
-                rows = to_rows(flat, lane)
+                rows = to_rows(flat)
                 for i in range(PACK):
                     q_rows[part, z, i] = rows[i]
                     even[part, z + 1, i] = last * rows[i]
@@ -434,6 +445,14 @@
     def _():
         landed[cut] = parts[cut % near, slab // groups]
 
+    for to in direct:
+        field_copy(to).wait_send()
+    if groups > 1:
+        for src in alike:
+            passed_on(src).wait_send()
+    for to in others:
+        for slot in range(per_group):
+            vector_copy(to, slot).wait_send()
     for o in range(n_cuts):
         c = (cut + o) % n_cuts
 
@@ -451,19 +470,13 @@
             arrive()
         else:
             pl.when(source_slab(c) != slab)(arrive)
-    total = landed[0]
-    for source in range(1, n_cuts):
-        total = total + landed[source]
-    out[...] = total
-
-    for to in direct:
-        field_copy(to).wait_send()
-    if groups > 1:
-        for src in alike:
-            passed_on(src).wait_send()
-    for to in others:
-        for slot in range(per_group):
-            vector_copy(to, slot).wait_send()
+    half = n_cuts // 2
+    for i, some in enumerate((range(half), range(half, n_cuts))):
+        total = jnp.zeros(landed.shape[1:], jnp.float32)
+        for source in some:
+            total = total + landed[source]
+        out[i, pl.ds(0, 2 * share_rows)] = total[: 2 * share_rows]
+
     for k in range(kept):
         if groups > 1:
             sibling_copy(k).wait_send()
@@ -475,7 +488,6 @@
     quasi, counts, slot_slice, occupation, filter_coef, trap_index, trap_table, mean_field, pairing
 ):
     n_cuts, nz = lax.axis_size("cuts"), lax.axis_size("slab")
-    cut = lax.axis_index("cuts")
     cap, flat = quasi.shape[1], quasi.shape[3]
     share = flat // n_cuts
     share_rows = share // NX
@@ -492,7 +504,7 @@
     slots = slot_slice.shape[0]
     sums = pl.pallas_call(
         functools.partial(kernel, dims),
-        out_shape=jax.ShapeDtypeStruct((rows, LANES), f32),
+        out_shape=jax.ShapeDtypeStruct((2, 3 * share_rows, LANES), f32),
         in_specs=[pl.BlockSpec(memory_space=pltpu.HBM)] * 8
         + [pl.BlockSpec(memory_space=pl.ANY)],
         out_specs=pl.BlockSpec(memory_space=pltpu.VMEM),
@@ -504,6 +516,8 @@
             pltpu.SMEM(trap_table.shape, f32),
             pltpu.VMEM(tall, i32),
             pltpu.VMEM(tall, f32),
+            pltpu.VMEM(tall, f32),
+            pltpu.VMEM((2, PACK, flat // (NX * PACK), LANES), f32),
             pltpu.VMEM((2, *tall), f32),
             pltpu.VMEM((per_group, nz, FLAT * width, 2, LANES), jnp.bfloat16),
             pltpu.VMEM((nz, 2, FLAT * width, LANES), f32),
@@ -541,10 +555,10 @@
         vectors,
     )
 
-    flat_sums = sums[: 2 * share_rows, :NX].reshape(2, share)
-    normal_density, anomalous_density = flat_sums[:1], flat_sums[1:]
-    mean_local = lax.dynamic_slice_in_dim(mean_field, cut * share, share, 1)
-    pairing_local = lax.dynamic_slice_in_dim(pairing, cut * share, share, 1)
+    halves = sums[:, :, :NX].reshape(6, share)
+    normal_density = halves[0:1] + halves[3:4]
+    anomalous_density = halves[1:2] + halves[4:5]
+    mean_local, pairing_local = halves[2:3], halves[5:6]
     cube_root = jnp.cbrt(normal_density + density_floor)
     new_mean_field = 0.5 * mean_local + 0.5 * (beta_coef * cube_root * cube_root - chem_level)
     new_pairing = 0.5 * pairing_local - coupling * anomalous_density

time: 25.8 us -> 24.5 us (0.950)
  other arithmetic: 1.35 us -> 0.67 us
  local copies, waits for them, and re-layouts: 1.53 us -> 0.86 us
    slice x3 -> x0, local copies, waits for them, and re-layouts: 0.94 us -> none  [body(): normal_density, anomalous_density = (flat_sums[:1], flat_sums[1:])]
    reshape x0 -> x1, local copies, waits for them, and re-layouts: none -> 0.86 us  [body(): halves = sums[:, :, :NX].reshape(6, share)]
    sub x1, other arithmetic: 1.35 us -> 0.67 us  [body(): new_pairing = 0.5 * pairing_local - coupling * anomalous_density]
    unnamed x4 -> x0, local copies, waits for them, and re-layouts: 0.59 us -> none
where the time goes in v4:
time: 24.5 us; the launch traced here: 24.2 us
  Pallas kernels  22.1 us (90%)
  local copies, waits for them, and re-layouts  0.86 us (4%)
  other arithmetic  0.67 us (3%)
  between operations  0.64 us (3%)
    pallas_call x1, Pallas kernels, body(): pl.pallas_call(functools.partial(kernel, dims), out_shape=jax.ShapeDtypeS...  22.1 us
    reshape x1, local copies, waits for them, and re-layouts, body(): halves = sums[:, :, :NX].reshape(6, share)  0.86 us
    sub x1, other arithmetic, body(): new_pairing = 0.5 * pairing_local - coupling * anomalous_density  0.67 us

profile of v4, /device:TPU:0, one launch (start us, length us, event | category | flops | bytes accessed | tf_op | source)
XLA Modules:
  0.0 24.2 jit_solution(5165272075504668174)
XLA Ops:
  0.6 22.1 %shard_map.120 = f32[2,36,128]{2,1,0:T(8,128)} custom-call(s32[8]{0:T(128)} %counts_in.1, s32[48]{0:T(128)} %slot_slice_in.1, f32[48]{0:T(128)} %occupation_in.1, f32[16,9]{1,0:T(8,128)} %coef_in.1, f32[32]{0:T(128)} %table_in.1, s32[72,128]{1,0:T(8,128)} %bitcast.9, f32[72,128]{1,0:T(8,128)} %bitcast.10, f32[72,128]{1,0:T(8,128)} %bitcast.11, ...), custom_call_target="tpu_custom_call" | custom-call | tf_op jit(solution)/shard_map/pallas_call | solution.py:505
  22.7 0.9 %reshape.27 = f32[6,1152]{1,0:T(8,128)S(1)} reshape(f32[2,36,96]{2,1,0:T(8,128)} %bitcast.8) | data formatting | bytes 55296 | tf_op jit(solution)/shard_map/reshape | solution.py:558
  23.6 0.7 %fusion.2 = (f32[1,1152]{1,0:T(1,128)}, f32[1,1152]{1,0:T(1,128)}, f32[1,1152]{1,0:T(1,128)}, f32[1,1152]{1,0:T(1,128)}) fusion(f32[6,1152]{1,0:T(8,128)S(1)} %reshape.27), kind=kLoop, calls=%fused_computation.4 | loop fusion | flops 11520 | bytes 46080 | tf_op jit(solution)/shard_map/sub | solution.py:564

commit v5 on v4

--- a/solution.py
+++ b/solution.py
@@ -23,6 +23,14 @@
 density_floor = 0.05
 
 MESH = pl.DeviceIdType.MESH
+
+
+def quotient(value, by):
+    return lax.div(value, jnp.int32(by))
+
+
+def modulo(value, by):
+    return lax.rem(value, jnp.int32(by))
 
 
 def round_up(value, step):
@@ -120,22 +128,22 @@
     cut, slab = lax.axis_index("cuts"), lax.axis_index("slab")
     near = n_cuts // pieces
     turn = max(near // 2, 1)
-    home = cut // near
+    home = quotient(cut, near)
     cap = per_group * groups
     kept = nz // groups
     halo = -(-DEGREE // PACK)
 
     def piece_of(s):
-        return (s // groups + cut // turn) % pieces
+        return modulo(quotient(s, groups) + quotient(cut, turn), pieces)
 
     def window_of(p):
         low = jnp.maximum(p * core - halo, 0)
-        return jnp.minimum(low // SUBLANES, windows - 1)
-
-    piece, group = piece_of(slab), slab % groups
+        return jnp.minimum(quotient(low, SUBLANES), windows - 1)
+
+    piece, group = piece_of(slab), modulo(slab, groups)
     keeps_own = (home == piece).astype(jnp.int32)
 
-    others = [(slab + o) % nz for o in range(1, nz)]
+    others = [modulo(slab + o, nz) for o in range(1, nz)]
     barrier = pltpu.get_barrier_semaphore()
     for to in others:
         pl.semaphore_signal(barrier, inc=1, device_id=(cut, to), device_id_type=MESH)
@@ -155,14 +163,14 @@
             ]
         )
     ]
-    for load in loads:
+    for load in loads[:4]:
         load.start()
 
     def source_slab(c):
-        return (home + pieces * n_cuts - c // turn) % pieces * groups + group
+        return modulo(home + pieces * n_cuts - quotient(c, turn), pieces) * groups + group
 
     for o in range(n_cuts):
-        c = (cut + o) % n_cuts
+        c = modulo(cut + o, n_cuts)
         s = source_slab(c)
 
         def greet(c=c, s=s):
@@ -210,7 +218,7 @@
     def vector_copy(to, slot):
         start = window_of(piece_of(to)) * (SUBLANES * FLAT)
         return pltpu.make_async_remote_copy(
-            src_ref=vectors.at[to % groups * per_group + slot, pl.ds(start, width * FLAT)],
+            src_ref=vectors.at[modulo(to, groups) * per_group + slot, pl.ds(start, width * FLAT)],
             dst_ref=got_q.at[slot, slab],
             send_sem=q_send.at[slot, to],
             recv_sem=q_recv.at[slot, slab],
@@ -219,7 +227,7 @@
         )
 
     window = window_of(piece)
-    alike = [(slab + o) % nz for o in range(groups, nz, groups)]
+    alike = [modulo(slab + o, nz) for o in range(groups, nz, groups)]
     direct = alike + ([mate] if groups > 1 else [])
     for to in direct:
         field_copy(to).start()
@@ -239,8 +247,12 @@
         )
 
     own_q(0).start()
+    for slot in range(1, per_group):
+        for to in others:
+            vector_copy(to, slot).start()
+        own_q(slot).start()
     for load in loads[4:]:
-        load.wait()
+        load.start()
 
     lane = lax.broadcasted_iota(jnp.int32, (width, LANES), 1)
     line = lax.broadcasted_iota(jnp.int32, (width, LANES), 0)
@@ -252,15 +264,6 @@
         buffer[:, 0] = blank
         buffer[:, nz + 1] = blank
     dens[...] = jnp.zeros(dens.shape, jnp.float32)
-
-    for part, here in enumerate((mean_here, pairing_here)):
-        count = here.shape[0] // FLAT
-        rows = to_rows([here[pl.ds(j, count, stride=FLAT)] for j in range(FLAT)])
-        for i in range(PACK):
-            local_rows[part, i] = rows[i]
-        for r in range(share_rows):
-            y = cut * share_rows + r
-            out[part, pl.ds(2 * share_rows + r, 1)] = local_rows[part, y % PACK, pl.ds(y // PACK, 1)]
 
     def wait_fields(src):
         pltpu.make_async_remote_copy(
@@ -276,15 +279,14 @@
         wait_fields(src)
         if groups > 1:
             passed_on(src).start()
-    for slot in range(1, per_group):
-        for to in others:
-            vector_copy(to, slot).start()
-        own_q(slot).start()
     own_f.wait()
     if groups > 1:
         wait_fields(mate)
         for src in alike:
             wait_fields(src + 1 - 2 * group)
+
+    for load in loads[4:]:
+        load.wait()
 
     def unpack_fields(z):
         for which in range(2):
@@ -443,7 +445,18 @@
 
     @pl.when(home == piece)
     def _():
-        landed[cut] = parts[cut % near, slab // groups]
+        landed[cut] = parts[modulo(cut, near), quotient(slab, groups)]
+
+    for part, here in enumerate((mean_here, pairing_here)):
+        count = here.shape[0] // FLAT
+        rows = to_rows([here[pl.ds(j, count, stride=FLAT)] for j in range(FLAT)])
+        for i in range(PACK):
+            local_rows[part, i] = rows[i]
+        for r in range(share_rows):
+            y = cut * share_rows + r
+            out[part, pl.ds(2 * share_rows + r, 1)] = local_rows[
+                part, modulo(y, PACK), pl.ds(quotient(y, PACK), 1)
+            ]
 
     for to in direct:
         field_copy(to).wait_send()
@@ -454,7 +467,7 @@
         for slot in range(per_group):
             vector_copy(to, slot).wait_send()
     for o in range(n_cuts):
-        c = (cut + o) % n_cuts
+        c = modulo(cut + o, n_cuts)
 
         def arrive(c=c):
             pltpu.make_async_remote_copy(

time: 24.5 us -> 24.4 us (level)
  no operation moved by 1% of the time
where the time goes in v5:
time: 24.4 us; the launch traced here: 24.2 us
  Pallas kernels  22 us (90%)
  local copies, waits for them, and re-layouts  0.86 us (4%)
  other arithmetic  0.67 us (3%)
  between operations  0.64 us (3%)
    pallas_call x1, Pallas kernels, body(): pl.pallas_call(functools.partial(kernel, dims), out_shape=jax.ShapeDtypeS...  22 us
    reshape x1, local copies, waits for them, and re-layouts, body(): halves = sums[:, :, :NX].reshape(6, share)  0.86 us
    sub x1, other arithmetic, body(): new_pairing = 0.5 * pairing_local - coupling * anomalous_density  0.67 us

profile of v5, /device:TPU:0, one launch (start us, length us, event | category | flops | bytes accessed | tf_op | source)
XLA Modules:
  0.0 24.2 jit_solution(13347455253798544982)
XLA Ops:
  0.6 22.0 %shard_map.120 = f32[2,36,128]{2,1,0:T(8,128)} custom-call(s32[8]{0:T(128)} %counts_in.1, s32[48]{0:T(128)} %slot_slice_in.1, f32[48]{0:T(128)} %occupation_in.1, f32[16,9]{1,0:T(8,128)} %coef_in.1, f32[32]{0:T(128)} %table_in.1, s32[72,128]{1,0:T(8,128)} %bitcast.9, f32[72,128]{1,0:T(8,128)} %bitcast.10, f32[72,128]{1,0:T(8,128)} %bitcast.11, ...), custom_call_target="tpu_custom_call" | custom-call | tf_op jit(solution)/shard_map/pallas_call | solution.py:518
  22.6 0.9 %reshape.27 = f32[6,1152]{1,0:T(8,128)S(1)} reshape(f32[2,36,96]{2,1,0:T(8,128)} %bitcast.8) | data formatting | bytes 55296 | tf_op jit(solution)/shard_map/reshape | solution.py:571
  23.5 0.7 %fusion.2 = (f32[1,1152]{1,0:T(1,128)}, f32[1,1152]{1,0:T(1,128)}, f32[1,1152]{1,0:T(1,128)}, f32[1,1152]{1,0:T(1,128)}) fusion(f32[6,1152]{1,0:T(8,128)S(1)} %reshape.27), kind=kLoop, calls=%fused_computation.4 | loop fusion | flops 11520 | bytes 46080 | tf_op jit(solution)/shard_map/sub | solution.py:577

commit v6 on v5

--- a/solution.py
+++ b/solution.py
@@ -307,7 +307,10 @@
         for i in range(PACK):
             around = pltpu.roll(rows[i], 1, 1) + pltpu.roll(rows[i], LANES - 1, 1)
             around = around + (padded[i] + padded[i + 2])
-            around = around + (ref[part, z, i] + ref[part, z + 2, i])
+            if not (isinstance(z, int) and z == 0):
+                around = around + ref[part, z, i]
+            if not (isinstance(z, int) and z == nz - 1):
+                around = around + ref[part, z + 2, i]
             sums.append(hop * around)
         return rows, sums
 
@@ -517,7 +520,7 @@
     slots = slot_slice.shape[0]
     sums = pl.pallas_call(
         functools.partial(kernel, dims),
-        out_shape=jax.ShapeDtypeStruct((2, 3 * share_rows, LANES), f32),
+        out_shape=pltpu.VMEM((2, 3 * share_rows, LANES), f32),
         in_specs=[pl.BlockSpec(memory_space=pltpu.HBM)] * 8
         + [pl.BlockSpec(memory_space=pl.ANY)],
         out_specs=pl.BlockSpec(memory_space=pltpu.VMEM),

time: 24.4 us -> 23 us (0.943)
  local copies, waits for them, and re-layouts: 0.86 us -> 0.08 us
  Pallas kernels: 22 us -> 21.4 us
    reshape x1, local copies, waits for them, and re-layouts: 0.86 us -> 0.08 us  [body(): halves = sums[:, :, :NX].reshape(6, share)]
    pallas_call x1, Pallas kernels: 22 us -> 21.4 us  [body(): pl.pallas_call(functools.partial(kernel, dims), out_shape=pltpu.VMEM((2,...]
where the time goes in v6:
time: 23 us; the launch traced here: 22.8 us
  Pallas kernels  21.4 us (93%)
  other arithmetic  0.67 us (3%)
  between operations  0.64 us (3%)
    pallas_call x1, Pallas kernels, body(): pl.pallas_call(functools.partial(kernel, dims), out_shape=pltpu.VMEM((2,...  21.4 us
    sub x1, other arithmetic, body(): new_pairing = 0.5 * pairing_local - coupling * anomalous_density  0.67 us

profile of v6, /device:TPU:0, one launch (start us, length us, event | category | flops | bytes accessed | tf_op | source)
XLA Modules:
  0.0 22.8 jit_solution(4007291395288566393)
XLA Ops:
  0.6 21.4 %shard_map.120 = f32[2,36,128]{2,1,0:T(8,128)S(1)} custom-call(s32[8]{0:T(128)} %counts_in.1, s32[48]{0:T(128)} %slot_slice_in.1, f32[48]{0:T(128)} %occupation_in.1, f32[16,9]{1,0:T(8,128)} %coef_in.1, f32[32]{0:T(128)} %table_in.1, s32[72,128]{1,0:T(8,128)} %bitcast.9, f32[72,128]{1,0:T(8,128)} %bitcast.10, f32[72,128]{1,0:T(8,128)} %bitcast.11, ...), custom_call_target="tpu_custom_call" | custom-call | tf_op jit(solution)/shard_map/pallas_call | solution.py:521
  22.0 0.1 reshape.27
  22.1 0.7 %fusion.2 = (f32[1,1152]{1,0:T(1,128)}, f32[1,1152]{1,0:T(1,128)}, f32[1,1152]{1,0:T(1,128)}, f32[1,1152]{1,0:T(1,128)}) fusion(f32[6,1152]{1,0:T(8,128)S(1)} %reshape.27), kind=kLoop, calls=%fused_computation.4 | loop fusion | flops 11520 | bytes 46080 | tf_op jit(solution)/shard_map/sub | solution.py:580

commit v7 on v6

--- a/solution.py
+++ b/solution.py
@@ -444,6 +444,7 @@
             sibling_copy(k).wait_recv()
         for c in range(near):
             pack(c, k)
+        for c in range(near):
             pl.when(elsewhere(c, k))(part_copy(c, k).start)
 
     @pl.when(home == piece)

time: 23 us -> 23 us (level)
  no operation moved by 1% of the time
where the time goes in v7:
time: 23 us; the launch traced here: 22.8 us
  Pallas kernels  21.4 us (93%)
  other arithmetic  0.67 us (3%)
  between operations  0.64 us (3%)
    pallas_call x1, Pallas kernels, body(): pl.pallas_call(functools.partial(kernel, dims), out_shape=pltpu.VMEM((2,...  21.4 us
    sub x1, other arithmetic, body(): new_pairing = 0.5 * pairing_local - coupling * anomalous_density  0.67 us

profile of v7, /device:TPU:0, one launch (start us, length us, event | category | flops | bytes accessed | tf_op | source)
XLA Modules:
  0.0 22.8 jit_solution(10520131246520584143)
XLA Ops:
  0.6 21.4 %shard_map.120 = f32[2,36,128]{2,1,0:T(8,128)S(1)} custom-call(s32[8]{0:T(128)} %counts_in.1, s32[48]{0:T(128)} %slot_slice_in.1, f32[48]{0:T(128)} %occupation_in.1, f32[16,9]{1,0:T(8,128)} %coef_in.1, f32[32]{0:T(128)} %table_in.1, s32[72,128]{1,0:T(8,128)} %bitcast.9, f32[72,128]{1,0:T(8,128)} %bitcast.10, f32[72,128]{1,0:T(8,128)} %bitcast.11, ...), custom_call_target="tpu_custom_call" | custom-call | tf_op jit(solution)/shard_map/pallas_call | solution.py:522
  22.0 0.1 reshape.27
  22.1 0.7 %fusion.2 = (f32[1,1152]{1,0:T(1,128)}, f32[1,1152]{1,0:T(1,128)}, f32[1,1152]{1,0:T(1,128)}, f32[1,1152]{1,0:T(1,128)}) fusion(f32[6,1152]{1,0:T(8,128)S(1)} %reshape.27), kind=kLoop, calls=%fused_computation.4 | loop fusion | flops 11520 | bytes 46080 | tf_op jit(solution)/shard_map/sub | solution.py:581
